TPU v7x, 128 devices: a whole 4x4x4 slice. The times are simulated.
128 devices in a mesh: row: 8 (over x_hi, y), col: 16 (over x_lo, z, core).
Axes of the slice: x: 4 (x_hi: 2, x_lo: 2; x = x_hi * 2 + x_lo), y: 4, z: 4, core: 2. Of those that a mesh axis runs over, the one named last changes fastest.
Arguments:
- vectors: float32 [100352, 2048], P(None, ('row', 'col')), may hold values from -6 to 6
- panels: float32 [2, 100352, 256], P(None, ('row', 'col')), may hold values from -0.078125 to 0.078125
- offsets: int32 [2], replicated, may hold values from 0 to 100096
- factor_upper: float32 [2, 256, 256], replicated, may hold values from -1 to 1
- scales: float32 [2, 256], replicated, may hold values from 1 to 2
Outputs:
- grid_vectors: float32 [100352, 2048], P('row', 'col')
All inputs are finite; a program needn't handle non-finite values.
Results may differ from a plain program's by a relative error of at most 0.00015.
Values sent between devices are 32-bit elements; how exact they have to be, the bound alone decides.
No kernel may reach another device: no remote copies, remote signals or barrier semaphores. Data moves between devices by JAX's collectives and lax.ppermute only.
A program may use at most 192 MiB of HBM per device.

v0:
```python
import jax
import jax.numpy as jnp
from jax import lax
from jax.experimental import pallas as pl
from jax.experimental.pallas import tpu as pltpu
from jax.sharding import PartitionSpec as P

NB = 64
F32 = jnp.float32
BF16 = jnp.bfloat16


def exact_dot(left, right):
    return jnp.dot(left, right, precision=lax.Precision.HIGHEST, preferred_element_type=F32)


def split(value):
    high = value.astype(BF16)
    return high, (value - high.astype(F32)).astype(BF16)


def masked(block, offset, row_index, grid_rows, first):
    rows, width = block.shape
    position = first + lax.broadcasted_iota(jnp.int32, (rows, 1), 0)
    row = (position // NB * grid_rows + row_index) * NB + position % NB
    begin = offset + lax.broadcasted_iota(jnp.int32, (1, width), 1)
    return jnp.where(row < begin, 0.0, jnp.where(row == begin, 1.0, block))


def deal_kernel(in_ref, out_ref, *, pairs):
    lane = lax.broadcasted_iota(jnp.int32, (in_ref.shape[0], 128), 1)
    low = lane < NB
    for q in range(pairs):
        for t in range(4):
            a = in_ref[:, pl.ds(2 * q * 512 + t * 128, 128)]
            b = in_ref[:, pl.ds((2 * q + 1) * 512 + t * 128, 128)]
            out_ref[2 * t, :, pl.ds(q * 128, 128)] = jnp.where(low, a, pltpu.roll(b, NB, 1))
            out_ref[2 * t + 1, :, pl.ds(q * 128, 128)] = jnp.where(low, pltpu.roll(a, NB, 1), b)


def deal(vectors_t, grid_rows):
    narrow, total = vectors_t.shape
    local = total // grid_rows
    steps = 7
    return pl.pallas_call(
        lambda i, o: deal_kernel(i, o, pairs=local // 128 // steps),
        grid=(steps,),
        in_specs=[pl.BlockSpec((narrow, total // steps), lambda s: (0, s))],
        out_specs=pl.BlockSpec((grid_rows, narrow, local // steps), lambda s: (0, 0, s)),
        out_shape=jax.ShapeDtypeStruct((grid_rows, narrow, local), F32),
    )(vectors_t)


def global_row(position, row_index, grid_rows):
    return (position // NB * grid_rows + row_index) * NB + position % NB


def start_block(info, views, held, sems, block, base, grid_rows):
    rows = views[0].shape[0]
    last = global_row(base + (block + 1) * rows - 1, info[2], grid_rows)
    for panel, view in enumerate(views):
        copy = pltpu.make_async_copy(
            view, held.at[panel, pl.ds(pl.multiple_of(block * rows, rows), rows)], sems.at[panel, block]
        )
        pl.when(last >= info[panel])(copy.start)


def wait_block(info, view, held, sems, block, base, grid_rows):
    rows = view.shape[0]
    last = global_row(base + (block + 1) * rows - 1, info[2], grid_rows)
    for panel in range(held.shape[0]):
        copy = pltpu.make_async_copy(
            view, held.at[panel, pl.ds(pl.multiple_of(block * rows, rows), rows)], sems.at[panel, block]
        )
        pl.when(last >= info[panel])(copy.wait)


def each_case(info, panel, first, rows, width, grid_rows, load, work):
    top = global_row(first, info[2], grid_rows)
    last = global_row(first + rows - 1, info[2], grid_rows)
    clear = top >= info[panel] + width

    @pl.when(clear)
    def _():
        work(load())

    @pl.when(jnp.logical_not(clear) & (last >= info[panel]))
    def _():
        work(masked(load(), info[panel], info[2], grid_rows, first))


def ring_block(info, step):
    return lax.rem(info[4] + step // 2, 4) * 2 + lax.rem(info[5] + step, 2)


def ring_sources(refs, info):
    return [(ring_block(info, step), [ref.at[k] for k in range(ref.shape[0])]) for step, ref in enumerate(refs)]


def gram_kernel(info, r_ref, *refs, grid_rows):
    *o_refs, total = refs
    panels, rows, width = r_ref.shape
    first = info[3] * rows
    zero, one = [split(masked(r_ref[k], info[k], info[2], grid_rows, first)) for k in range(panels)]
    dims = (((0,), (0,)), ((), ()))

    def dot(left, right):
        return lax.dot_general(left, right, dims, preferred_element_type=F32)

    total[...] = dot(one[0], zero[0]) + (dot(one[0], zero[1]) + dot(one[1], zero[0]))
    part = width // len(o_refs)
    for step, o_ref in enumerate(o_refs):
        at = lax.rem(info[4] + step, len(o_refs)) * part
        o_ref[...] = total[pl.ds(pl.multiple_of(at, part), part), :]


def gram_parts(info, panels, parts, grid_rows):
    width = panels.shape[2]
    return pl.pallas_call(
        lambda *refs: gram_kernel(*refs, grid_rows=grid_rows),
        in_specs=[pl.BlockSpec(memory_space=pltpu.SMEM), pl.BlockSpec(memory_space=pltpu.VMEM)],
        out_specs=[pl.BlockSpec(memory_space=pltpu.VMEM)] * parts,
        out_shape=[jax.ShapeDtypeStruct((width // parts, width), F32)] * parts,
        scratch_shapes=[pltpu.VMEM((width, width), F32)],
        compiler_params=pltpu.CompilerParams(vmem_limit_bytes=16 * 1024 * 1024),
    )(info, panels)


def inner_kernel(info, v_ref, w_ref, *refs, count, grid_rows, chunk):
    *r_refs, o_ref, held, sems = refs
    narrow = v_ref.shape[0]
    panels, total, width = held.shape
    sources = ring_sources(r_refs, info)
    base = info[3] * total
    for block, views in sources:
        start_block(info, views, held, sems, block, base, grid_rows)
    o_ref[...] = w_ref[...]
    view = sources[0][1][0]
    wait_block(info, view, held, sems, 0, base, grid_rows)

    def step(q, carry):
        wait_block(info, view, held, sems, q + 1, base, grid_rows)
        at = pl.multiple_of(q * chunk, chunk)
        first = base + at
        for k in range(panels):

            def work(block, k=k):
                high, low = split(block)
                v_high, v_low = split(v_ref[:, pl.ds(pl.multiple_of(first, 128), chunk)])
                both = jnp.concatenate([v_high, v_low], axis=0)
                main = jnp.dot(both, high, preferred_element_type=F32)
                rest = jnp.dot(v_high, low, preferred_element_type=F32)
                o_ref[:, k * width : (k + 1) * width] += main[:narrow] + (main[narrow:] + rest)

            each_case(info, k, first, chunk, width, grid_rows, lambda k=k: held[k, pl.ds(at, chunk), :], work)
        return carry

    lax.fori_loop(0, count - 1, step, 0)


def inner(info, v, start, gathered, count, shape, grid_rows):
    panels, rows, width = shape
    narrow = v.shape[0]
    total = count * rows
    vmem = pl.BlockSpec(memory_space=pltpu.VMEM)
    return pl.pallas_call(
        lambda *refs: inner_kernel(*refs, count=count, grid_rows=grid_rows, chunk=total // (count - 1)),
        in_specs=[pl.BlockSpec(memory_space=pltpu.SMEM), vmem, vmem]
        + [pl.BlockSpec(memory_space=pltpu.HBM)] * len(gathered),
        out_specs=vmem,
        out_shape=jax.ShapeDtypeStruct((narrow, panels * width), F32),
        scratch_shapes=[
            pltpu.VMEM((panels, total, width), F32),
            pltpu.SemaphoreType.DMA((panels, count)),
        ],
        compiler_params=pltpu.CompilerParams(vmem_limit_bytes=50 * 1024 * 1024),
        cost_estimate=pl.CostEstimate(
            flops=6 * narrow * panels * total * width, bytes_accessed=4 * panels * total * width, transcendentals=0
        ),
    )(info, v, start, *gathered)


def solve_kernel(parts_ref, mix_ref, out_ref):
    total = parts_ref[0]
    for i in range(1, parts_ref.shape[0]):
        total += parts_ref[i]
    solved = jnp.dot(total, mix_ref[...], precision=lax.Precision.HIGHEST, preferred_element_type=F32)
    for i in range(parts_ref.shape[0]):
        out_ref[i] = solved


def solve(parts, mix):
    return pl.pallas_call(
        solve_kernel, out_shape=jax.ShapeDtypeStruct(parts.shape, F32)
    )(parts, mix)


def mixing_kernel(upper_ref, scales_ref, gram_ref, o_ref):
    width = scales_ref.shape[1]
    gram = (gram_ref[:4] + gram_ref[4:]).reshape(width, width)
    row = lax.broadcasted_iota(jnp.int32, (width, width), 0)
    column = lax.broadcasted_iota(jnp.int32, (width, width), 1)

    def factor(k):
        diagonal = jnp.where(row == column, scales_ref[k : k + 1, :], 0.0)
        return jnp.where(row < column, upper_ref[k], diagonal)

    zero, one = factor(0), factor(1)
    corner = exact_dot(one, exact_dot(gram, zero))
    o_ref[:width, :width] = zero.T
    o_ref[:width, width:] = -corner.T
    o_ref[width:, :width] = jnp.zeros((width, width), F32)
    o_ref[width:, width:] = one.T


def mixing(factor_upper, scales, gram):
    panels, width = scales.shape
    return pl.pallas_call(
        mixing_kernel,
        out_shape=jax.ShapeDtypeStruct((panels * width, panels * width), F32),
        compiler_params=pltpu.CompilerParams(vmem_limit_bytes=16 * 1024 * 1024),
    )(factor_upper, scales, gram)


def apply_kernel(info, v_ref, t_ref, *refs, count, grid_rows):
    *r_refs, o_ref, t_scr, held, moving, sems, v_sems, o_sems = refs
    panels, total, width = held.shape
    narrow = t_ref.shape[0]
    rows = total // (2 * count)
    sources = [(info[3] * count + block, views) for block, views in ring_sources(r_refs[:count], info)]
    sources += [((1 - info[3]) * count + block, views) for block, views in ring_sources(r_refs[count:], info)]

    def place(block):
        return pl.ds(pl.multiple_of(block * rows, rows), rows)

    def v_copy(block):
        return pltpu.make_async_copy(v_ref.at[place(block)], moving.at[place(block)], v_sems.at[block])

    def o_copy(block):
        return pltpu.make_async_copy(moving.at[place(block)], o_ref.at[place(block)], o_sems.at[block])

    for block, views in sources:
        v_copy(block).start()
        start_block(info, views, held, sems, block, 0, grid_rows)
    for k in range(panels):
        high, low = split(t_ref[:, k * width : (k + 1) * width].T)
        t_scr[k, :, :narrow] = high
        t_scr[k, :, narrow:] = low

    def step(done, carry):
        half = jnp.where(done < count, info[3], 1 - info[3])
        block = half * count + ring_block(info, lax.rem(done, count))
        first = block * rows
        v_copy(block).wait()
        wait_block(info, sources[0][1][0], held, sems, block, 0, grid_rows)
        for k in range(panels):

            def work(value, k=k):
                high, low = split(value)
                main = jnp.dot(high, t_scr[k], preferred_element_type=F32)
                rest = jnp.dot(low, t_scr[k, :, :narrow], preferred_element_type=F32)
                moving[place(block), :] -= main[:, :narrow] + (main[:, narrow:] + rest)

            each_case(info, k, first, rows, width, grid_rows, lambda k=k: held[k, place(block), :], work)
        o_copy(block).start()
        return carry

    lax.fori_loop(0, 2 * count, step, 0)
    for block in range(2 * count):
        o_copy(block).wait()


def apply(info, v, t, gathered, count, shape, grid_rows):
    panels, rows, width = shape
    narrow = v.shape[1]
    total = 2 * count * rows
    anywhere = pl.BlockSpec(memory_space=pltpu.HBM)
    return pl.pallas_call(
        lambda *refs: apply_kernel(*refs, count=count, grid_rows=grid_rows),
        in_specs=[pl.BlockSpec(memory_space=pltpu.SMEM), anywhere, pl.BlockSpec(memory_space=pltpu.VMEM)]
        + [anywhere] * len(gathered),
        out_specs=anywhere,
        out_shape=jax.ShapeDtypeStruct(v.shape, F32),
        scratch_shapes=[
            pltpu.VMEM((panels, width, 2 * narrow), BF16),
            pltpu.VMEM((panels, total, width), F32),
            pltpu.VMEM((total, narrow), F32),
            pltpu.SemaphoreType.DMA((panels, 2 * count)),
            pltpu.SemaphoreType.DMA((2 * count,)),
            pltpu.SemaphoreType.DMA((2 * count,)),
        ],
        compiler_params=pltpu.CompilerParams(vmem_limit_bytes=56 * 1024 * 1024),
        cost_estimate=pl.CostEstimate(
            flops=6 * narrow * panels * total * width, bytes_accessed=4 * panels * total * width, transcendentals=0
        ),
    )(info, v, t, *gathered)


def shards(vectors, panels, offsets, factor_upper, scales):
    grid_rows, grid_cols = lax.axis_size("row"), lax.axis_size("col")
    row_index, col_index = lax.axis_index("row"), lax.axis_index("col")
    half = grid_cols // 2
    rows, width = panels.shape[1:]
    narrow = vectors.shape[1]
    side, ring, core = col_index // half, col_index // 2 % 4, col_index % 2

    def along_col(value, to):
        return lax.ppermute(value, "col", [(c, to(c)) for c in range(grid_cols)])

    def along_row(value, to):
        return lax.ppermute(value, "row", [(r, to(r)) for r in range(grid_rows)])

    def up(c):
        return c // 8 * 8 + (c + 2) % 8

    def down(c):
        return c // 8 * 8 + (c + 6) % 8

    def across(value):
        return along_col(value, lambda c: c ^ 1)

    def info(*ints):
        return jnp.stack([offsets[0], offsets[1]] + [i.astype(jnp.int32) for i in (row_index, *ints)])

    def shifted(step):
        return lambda r: r // 4 * 4 + (r + step) % 4

    def turned(step):
        return lambda c: c // 8 * 8 + (c + 2 * step) % 8

    below, above = along_col(panels, up), along_col(panels, down)
    near = along_col(panels, lambda c: c ^ half)
    panels_across = across(panels)

    dealt = deal(vectors.T, grid_rows)
    level = row_index % 4
    gram, *parts = gram_parts(info(col_index, level), panels, 4, grid_rows)
    gram = sum([along_row(parts[step - 1], shifted(step)) for step in (1, 2, 3)], gram)
    gram = gram.reshape(2, width // 8, width)
    given = across(lax.dynamic_index_in_dim(gram, 1 - core, 0, False))
    gram = lax.dynamic_index_in_dim(gram, core, 0, False) + given
    gram = gram + along_col(gram, lambda c: c ^ half)
    below, above, near, dealt, gram, panels_across = lax.optimization_barrier(
        (below, above, near, dealt, gram, panels_across)
    )

    far = along_col(below, up)
    other_above = along_col(near, down)
    moved = lax.all_to_all(dealt, "row", 0, 0, tiled=True).reshape(grid_rows * narrow, -1)
    crossed = [across(below), across(above), across(near)]
    gram, *crossed = lax.optimization_barrier((gram, *crossed))
    below_across, above_across, near_across = crossed
    gram = sum([along_col(gram, turned(step)) for step in (1, 2, 3)], gram)
    other_above, far, near, gram = lax.optimization_barrier((other_above, far, near, gram))

    other_below, other_far = along_col(near, up), along_col(other_above, down)
    other_above_across, far_across = across(other_above), across(far)
    given = across(gram)
    gram = jnp.where(core == 0, jnp.concatenate([gram, given]), jnp.concatenate([given, gram]))
    moved, gram, other_above_across, far_across = lax.optimization_barrier(
        (moved, gram, other_above_across, far_across)
    )

    own = [panels, panels_across, above, above_across, far, far_across, below, below_across]
    start = jnp.zeros((grid_rows * narrow, 2 * width), F32)
    sums = inner(info(side, ring, core), moved, start, own, half, panels.shape, grid_rows)
    sums, gram, other_far, other_below = lax.optimization_barrier((sums, gram, other_far, other_below))
    other = [near, near_across, other_above, other_above_across]
    other += [other_far, across(other_far), other_below, across(other_below)]
    gram = jnp.broadcast_to(gram[None], (grid_rows,) + gram.shape)
    gram = lax.all_to_all(gram, "row", 0, 0, tiled=True)
    mix = mixing(factor_upper, scales, gram)

    sums = inner(info(1 - side, ring, core), moved, sums, other, half, panels.shape, grid_rows)
    parts = lax.all_to_all(sums.reshape(grid_rows, narrow, 2 * width), "row", 0, 0, tiled=True)
    solved = solve(parts, mix)
    solved = lax.all_to_all(solved, "row", 0, 0, tiled=True).reshape(grid_rows * narrow, 2 * width)
    return apply(info(side, ring, core), moved.T, solved, own + other, half, panels.shape, grid_rows)


def solution(mesh):
    return jax.shard_map(
        shards,
        mesh=mesh,
        in_specs=(P(None, ("row", "col")), P(None, ("row", "col"), None), P(), P(), P()),
        out_specs=P("row", "col"),
        check_vma=False,
    )
```

profile of v0, /device:TPU:0, one launch (start us, length us, event | category | flops | bytes accessed | tf_op | source)
XLA Modules:
  0.0 201.0 jit_solution(16133567127287563327)
XLA Ops:
  0.0 2.0 collective-permute-start
  2.0 2.1 %collective-permute-start.1 = (f32[2,784,256]{2,1,0:T(8,128)}, f32[2,784,256]{2,1,0:T(8,128)}, u32[]{:S(2)}, u32[]{:S(2)}) collective-permute-start(f32[2,784,256]{2,1,0:T(8,128)} %refs_3_.3), channel_id=1, source_target_pairs={{0,6},{1,7},{2,0},{3,1},{4,2},{5,3},{6,4},{7,5},{8,14},{9,15},{10,... | collective-permute-start | bytes 4816904 | tf_op jit(solution)/shard_map/ppermute | solution.py:308
  4.1 1.5 collective-permute-start.2
  6.4 1.4 copy-done
  7.8 1.8 shard_map.56
  9.6 1.6 collective-permute-start.3
  11.2 4.2 %collective-permute-done.3 = f32[64,256]{1,0:T(8,128)S(1)} collective-permute-done((f32[64,256]{1,0:T(8,128)S(1)}, f32[64,256]{1,0:T(8,128)S(1)}, u32[]{:S(2)}, u32[]{:S(2)}) %collective-permute-start.3) | collective-permute-done | bytes 65568 | tf_op jit(solution)/shard_map/ppermute | solution.py:311
  15.4 1.9 collective-permute-start.4
  17.3 3.9 %collective-permute-done.4 = f32[64,256]{1,0:T(8,128)S(1)} collective-permute-done((f32[64,256]{1,0:T(8,128)S(1)}, f32[64,256]{1,0:T(8,128)S(1)}, u32[]{:S(2)}, u32[]{:S(2)}) %collective-permute-start.4) | collective-permute-done | bytes 65568 | tf_op jit(solution)/shard_map/ppermute | solution.py:311
  21.2 1.7 collective-permute-start.5
  22.9 2.5 %collective-permute-done.5 = f32[64,256]{1,0:T(8,128)S(1)} collective-permute-done((f32[64,256]{1,0:T(8,128)S(1)}, f32[64,256]{1,0:T(8,128)S(1)}, u32[]{:S(2)}, u32[]{:S(2)}) %collective-permute-start.5) | collective-permute-done | bytes 65568 | tf_op jit(solution)/shard_map/ppermute | solution.py:311
  27.3 8.9 %shard_map.55 = f32[8,16,12544]{2,1,0:T(8,128)} custom-call(f32[16,100352]{1,0:T(8,128)} %bitcast.19), custom_call_target="tpu_custom_call" | custom-call | tf_op jit(solution)/shard_map/pallas_call | solution.py:45
  36.2 5.4 %collective-permute-done.7 = f32[32,256]{1,0:T(8,128)S(1)} collective-permute-done((f32[32,256]{1,0:T(8,128)S(1)}, f32[32,256]{1,0:T(8,128)S(1)}, u32[]{:S(2)}, u32[]{:S(2)}) %collective-permute-start.7) | collective-permute-done | bytes 32800 | tf_op jit(solution)/shard_map/ppermute | solution.py:308
  42.9 7.1 %all-to-all-start = ((f32[8,16,12544]{2,1,0:T(8,128)}), f32[8,16,12544]{2,1,0:T(8,128)}, u32[]{:S(2)}, u32[]{:S(2)}) async-start(f32[8,16,12544]{2,1,0:T(8,128)} %shard_map.55), calls=%async_computation | async-start | bytes 12845056 | tf_op jit(solution)/shard_map/all_to_all | solution.py:349
  50.5 3.2 %collective-permute-start.9 = (f32[2,784,256]{2,1,0:T(8,128)S(1)}, f32[2,784,256]{2,1,0:T(8,128)}, u32[]{:S(2)}, u32[]{:S(2)}) collective-permute-start(f32[2,784,256]{2,1,0:T(8,128)S(1)} %collective-permute-done.2.refs_3_.refs_11_), channel_id=1, source_target_pairs={{0,6},{1,7},{2,0},{3,1},{4,2},{5,3},{6,4},{7,5},{8,14},{9,15},{10,... | collective-permute-start | bytes 4816904 | tf_op jit(solution)/shard_map/ppermute | solution.py:308
  53.8 4.4 %collective-permute-done.12.refs_6_ = f32[2,784,256]{2,1,0:T(8,128)S(1)} collective-permute-done((f32[2,784,256]{2,1,0:T(8,128)}, f32[2,784,256]{2,1,0:T(8,128)S(1)}, u32[]{:S(2)}, u32[]{:S(2)}) %collective-permute-start.12) | collective-permute-done | bytes 1605664 | tf_op jit(solution)/shard_map/ppermute | solution.py:308
  59.9 2.7 %collective-permute-start.15 = (f32[32,256]{1,0:T(8,128)S(1)}, f32[32,256]{1,0:T(8,128)S(1)}, u32[]{:S(2)}, u32[]{:S(2)}) collective-permute-start(f32[32,256]{1,0:T(8,128)S(1)} %add.53), channel_id=1, source_target_pairs={{0,4},{1,5},{2,6},{3,7},{4,0},{5,1},{6,2},{7,3},{8,12},{9,13},{10,... | collective-permute-start | bytes 98312 | tf_op jit(solution)/shard_map/ppermute | solution.py:308
  63.6 26.9 %collective-permute-done.14 = f32[32,256]{1,0:T(8,128)S(1)} collective-permute-done((f32[32,256]{1,0:T(8,128)S(1)}, f32[32,256]{1,0:T(8,128)S(1)}, u32[]{:S(2)}, u32[]{:S(2)}) %collective-permute-start.14) | collective-permute-done | bytes 32800 | tf_op jit(solution)/shard_map/ppermute | solution.py:308
  91.4 2.7 %collective-permute-start.20 = (f32[2,784,256]{2,1,0:T(8,128)}, f32[2,784,256]{2,1,0:T(8,128)}, u32[]{:S(2)}, u32[]{:S(2)}) collective-permute-start(f32[2,784,256]{2,1,0:T(8,128)} %collective-permute-done.9.refs_5_.refs_13_), channel_id=1, source_target_pairs={{0,6},{1,7},{2,0},{3,1},{4,2},{5,3},{6,4},{7,5},{8,14},{9,15},{10,... | collective-permute-start | bytes 4816904 | tf_op jit(solution)/shard_map/ppermute | solution.py:308
  94.3 2.4 %collective-permute-done.17 = f32[32,256]{1,0:T(8,128)S(1)} collective-permute-done((f32[32,256]{1,0:T(8,128)S(1)}, f32[32,256]{1,0:T(8,128)S(1)}, u32[]{:S(2)}, u32[]{:S(2)}) %collective-permute-start.17) | collective-permute-done | bytes 32800 | tf_op jit(solution)/shard_map/ppermute | solution.py:308
  97.0 24.6 %all-to-all-done = f32[8,16,12544]{2,1,0:T(8,128)} async-done(((f32[8,16,12544]{2,1,0:T(8,128)}), f32[8,16,12544]{2,1,0:T(8,128)}, u32[]{:S(2)}, u32[]{:S(2)}) %all-to-all-start) | async-done | bytes 6422560 | tf_op jit(solution)/shard_map/all_to_all | solution.py:349
  121.7 1.4 copy-done.4
  123.1 8.9 %shard_map.57.refs_2_ = f32[128,512]{1,0:T(8,128)S(1)} custom-call(s32[6]{0:T(128)S(1)} %stack.43.refs_0_, f32[128,12544]{1,0:T(8,128)} %bitcast.10.refs_1_, f32[128,512]{1,0:T(8,128)S(1)} %broadcast_in_dim.4.refs_2_, f32[2,784,256]{2,1,0:T(8,128)S(1)} %copy-done.1, f32[2,784,256]{2,1,0:T(8,128)S(1)} %copy-done.4, ...), custom_call_target="tpu_custom_call" | custom-call | flops 2466250752 | bytes 12845056 | tf_op jit(solution)/shard_map/pallas_call | solution.py:166
  133.7 7.2 %all-to-all-start.2 = ((f32[8,64,256]{2,1,0:T(8,128)}), f32[8,64,256]{2,1,0:T(8,128)}, u32[]{:S(2)}, u32[]{:S(2)}) async-start(f32[8,64,256]{2,1,0:T(8,128)} %broadcast_in_dim.10), calls=%async_computation.2 | async-start | bytes 1048576 | tf_op jit(solution)/shard_map/all_to_all | solution.py:371
  141.0 9.5 %shard_map.58 = f32[128,512]{1,0:T(8,128)S(1)} custom-call(s32[6]{0:T(128)S(1)} %stack.48.refs_0_, f32[128,12544]{1,0:T(8,128)} %bitcast.10.refs_1_, f32[128,512]{1,0:T(8,128)S(1)} %shard_map.57.refs_2_, f32[2,784,256]{2,1,0:T(8,128)S(1)} %collective-permute-done.2.refs_3_.refs_11_, f32[2,784,256]{2,1,0:T(8,128)S(1)} %copy-done.6, ...), custom_call_target="tpu_custom_call" | custom-call | flops 2466250752 | bytes 12845056 | tf_op jit(solution)/shard_map/pallas_call | solution.py:166
  152.0 6.4 %all-to-all-start.1 = ((f32[8,16,512]{2,1,0:T(8,128)}), f32[8,16,512]{2,1,0:T(8,128)S(1)}, u32[]{:S(2)}, u32[]{:S(2)}) async-start(f32[8,16,512]{2,1,0:T(8,128)} %bitcast.17), calls=%async_computation.1 | async-start | bytes 524288 | tf_op jit(solution)/shard_map/all_to_all | solution.py:375
  159.5 2.3 %shard_map.59.mix_ref = f32[512,512]{1,0:T(8,128)S(1)} custom-call(f32[2,256,256]{2,1,0:T(8,128)S(1)} %copy-done.9, f32[2,256]{1,0:T(2,128)S(1)} %copy-done.11, f32[8,64,256]{2,1,0:T(8,128)} %all-to-all-done.2.gram_ref), custom_call_target="tpu_custom_call" | custom-call | tf_op jit(solution)/shard_map/pallas_call | solution.py:218
  162.7 4.5 %all-to-all-done.1.parts_ref = f32[8,16,512]{2,1,0:T(8,128)S(1)} async-done(((f32[8,16,512]{2,1,0:T(8,128)}), f32[8,16,512]{2,1,0:T(8,128)S(1)}, u32[]{:S(2)}, u32[]{:S(2)}) %all-to-all-start.1) | async-done | bytes 262176 | tf_op jit(solution)/shard_map/all_to_all | solution.py:375
  168.0 2.6 %shard_map.60 = f32[8,16,512]{2,1,0:T(8,128)} custom-call(f32[8,16,512]{2,1,0:T(8,128)} %copy-done.15, f32[512,512]{1,0:T(8,128)} %copy-done.7), custom_call_target="tpu_custom_call" | custom-call | tf_op jit(solution)/shard_map/pallas_call | solution.py:193
  170.6 3.4 %all-to-all-start.3 = ((f32[8,16,512]{2,1,0:T(8,128)}), f32[8,16,512]{2,1,0:T(8,128)S(1)}, u32[]{:S(2)}, u32[]{:S(2)}) async-start(f32[8,16,512]{2,1,0:T(8,128)} %shard_map.60), calls=%async_computation.3 | async-start | bytes 524288 | tf_op jit(solution)/shard_map/all_to_all | solution.py:377
  174.0 8.0 %copy.9 = f32[128,12544]{0,1:T(8,128)} copy(f32[128,12544]{1,0:T(8,128)} %bitcast.10.refs_1_) | data formatting | bytes 12845056 | tf_op jit(solution)/shard_map/optimization_barrier | solution.py:360
  183.4 17.5 %shard_map.61 = f32[12544,128]{1,0:T(8,128)} custom-call(s32[6]{0:T(128)} %copy-done.10, f32[12544,128]{1,0:T(8,128)} %bitcast.18, f32[128,512]{1,0:T(8,128)} %bitcast.20, f32[2,784,256]{2,1,0:T(8,128)} %refs_3_.3, f32[2,784,256]{2,1,0:T(8,128)} %copy-done.3, f32[2,784,256]{2,1,0:T(8,128)} %collective-permute-done.1.refs_5_, f32[2,784,256]{2,1,0:T(8,128)} %copy-done.13, ...), custom_call_target="tpu_custom_call" | custom-call | flops 4932501504 | bytes 25690112 | tf_op jit(solution)/shard_map/pallas_call | solution.py:278
  (77 shorter events, 15.7 us)
Async XLA Ops:
  0.0 41.6 %collective-permute-start = (f32[2,784,256]{2,1,0:T(8,128)}, f32[2,784,256]{2,1,0:T(8,128)}, u32[]{:S(2)}, u32[]{:S(2)}) collective-permute-start(f32[2,784,256]{2,1,0:T(8,128)} %refs_3_.3), channel_id=1, source_target_pairs={{0,2},{1,3},{2,4},{3,5},{4,6},{5,7},{6,0},{7,1},{8,10},{9,11},{10,... | collective-permute-start | bytes 4816904 | tf_op jit(solution)/shard_map/ppermute | solution.py:308
  2.0 39.6 %collective-permute-start.1 = (f32[2,784,256]{2,1,0:T(8,128)}, f32[2,784,256]{2,1,0:T(8,128)}, u32[]{:S(2)}, u32[]{:S(2)}) collective-permute-start(f32[2,784,256]{2,1,0:T(8,128)} %refs_3_.3), channel_id=1, source_target_pairs={{0,6},{1,7},{2,0},{3,1},{4,2},{5,3},{6,4},{7,5},{8,14},{9,15},{10,... | collective-permute-start | bytes 4816904 | tf_op jit(solution)/shard_map/ppermute | solution.py:308
  4.1 37.5 %collective-permute-start.2 = (f32[2,784,256]{2,1,0:T(8,128)}, f32[2,784,256]{2,1,0:T(8,128)S(1)}, u32[]{:S(2)}, u32[]{:S(2)}) collective-permute-start(f32[2,784,256]{2,1,0:T(8,128)} %refs_3_.3), channel_id=1, source_target_pairs={{0,8},{1,9},{2,10},{3,11},{4,12},{5,13},{6,14},{7,15},{8,0},{9,1},... | collective-permute-start | bytes 4816904 | tf_op jit(solution)/shard_map/ppermute | solution.py:308
  5.6 36.0 %collective-permute-start.8 = (f32[2,784,256]{2,1,0:T(8,128)}, f32[2,784,256]{2,1,0:T(8,128)S(1)}, u32[]{:S(2)}, u32[]{:S(2)}) collective-permute-start(f32[2,784,256]{2,1,0:T(8,128)} %refs_3_.3), channel_id=1, source_target_pairs={{0,1},{1,0},{2,3},{3,2},{4,5},{5,4},{6,7},{7,6},{8,9},{9,8},{10,11... | collective-permute-start | bytes 4816904 | tf_op jit(solution)/shard_map/ppermute | solution.py:308
  9.6 5.8 %collective-permute-start.3 = (f32[64,256]{1,0:T(8,128)S(1)}, f32[64,256]{1,0:T(8,128)S(1)}, u32[]{:S(2)}, u32[]{:S(2)}) collective-permute-start(f32[64,256]{1,0:T(8,128)S(1)} %get-tuple-element.32), channel_id=1, source_target_pairs={{0,16},{16,32},{32,48},{48,0},{64,80},{80,96},{96,112},{112,64},{1... | collective-permute-start | bytes 196616 | tf_op jit(solution)/shard_map/ppermute | solution.py:311
  15.4 5.8 %collective-permute-start.4 = (f32[64,256]{1,0:T(8,128)S(1)}, f32[64,256]{1,0:T(8,128)S(1)}, u32[]{:S(2)}, u32[]{:S(2)}) collective-permute-start(f32[64,256]{1,0:T(8,128)S(1)} %get-tuple-element.33), channel_id=1, source_target_pairs={{0,32},{16,48},{32,0},{48,16},{64,96},{80,112},{96,64},{112,80},{1... | collective-permute-start | bytes 196616 | tf_op jit(solution)/shard_map/ppermute | solution.py:311
  21.2 4.3 %collective-permute-start.5 = (f32[64,256]{1,0:T(8,128)S(1)}, f32[64,256]{1,0:T(8,128)S(1)}, u32[]{:S(2)}, u32[]{:S(2)}) collective-permute-start(f32[64,256]{1,0:T(8,128)S(1)} %get-tuple-element.34), channel_id=1, source_target_pairs={{0,48},{16,0},{32,16},{48,32},{64,112},{80,64},{96,80},{112,96},{1... | collective-permute-start | bytes 196616 | tf_op jit(solution)/shard_map/ppermute | solution.py:311
  25.5 1.3 collective-permute-start.6
  26.8 14.8 %collective-permute-start.7 = (f32[32,256]{1,0:T(8,128)S(1)}, f32[32,256]{1,0:T(8,128)S(1)}, u32[]{:S(2)}, u32[]{:S(2)}) collective-permute-start(f32[32,256]{1,0:T(8,128)S(1)} %bitcast_add_fusion), channel_id=1, source_target_pairs={{0,8},{1,9},{2,10},{3,11},{4,12},{5,13},{6,14},{7,15},{8,0},{9,1},... | collective-permute-start | bytes 98312 | tf_op jit(solution)/shard_map/ppermute | solution.py:308
  41.6 52.6 %copy-start.16 = (s32[2]{0:T(128)S(1)}, s32[2]{0:T(128)}, u32[]{:S(2)}) copy-start(s32[2]{0:T(128)} %param.7) | copy-start | bytes 28
  41.6 99.3 %copy-start.2 = (f32[2,784,256]{2,1,0:T(8,128)}, f32[2,784,256]{2,1,0:T(8,128)S(1)}, u32[]{:S(2)}) copy-start(f32[2,784,256]{2,1,0:T(8,128)S(1)} %collective-permute-done.2.refs_3_.refs_11_) | copy-start | bytes 4816900
  42.9 78.8 %copy-start.1 = (f32[2,784,256]{2,1,0:T(8,128)S(1)}, f32[2,784,256]{2,1,0:T(8,128)}, u32[]{:S(2)}) copy-start(f32[2,784,256]{2,1,0:T(8,128)} %refs_3_.3) | copy-start | bytes 4816900
  42.9 78.7 %all-to-all-start = ((f32[8,16,12544]{2,1,0:T(8,128)}), f32[8,16,12544]{2,1,0:T(8,128)}, u32[]{:S(2)}, u32[]{:S(2)}) async-start(f32[8,16,12544]{2,1,0:T(8,128)} %shard_map.55), calls=%async_computation | async-start | bytes 12845056 | tf_op jit(solution)/shard_map/all_to_all | solution.py:349
  49.9 3.8 %collective-permute-start.11 = (f32[2,784,256]{2,1,0:T(8,128)}, f32[2,784,256]{2,1,0:T(8,128)S(1)}, u32[]{:S(2)}, u32[]{:S(2)}) collective-permute-start(f32[2,784,256]{2,1,0:T(8,128)} %collective-permute-done.refs_9_), channel_id=1, source_target_pairs={{0,1},{1,0},{2,3},{3,2},{4,5},{5,4},{6,7},{7,6},{8,9},{9,8},{10,11... | collective-permute-start | bytes 4816904 | tf_op jit(solution)/shard_map/ppermute | solution.py:308
  49.9 8.3 %collective-permute-start.12 = (f32[2,784,256]{2,1,0:T(8,128)}, f32[2,784,256]{2,1,0:T(8,128)S(1)}, u32[]{:S(2)}, u32[]{:S(2)}) collective-permute-start(f32[2,784,256]{2,1,0:T(8,128)} %collective-permute-done.1.refs_5_), channel_id=1, source_target_pairs={{0,1},{1,0},{2,3},{3,2},{4,5},{5,4},{6,7},{7,6},{8,9},{9,8},{10,11... | collective-permute-start | bytes 4816904 | tf_op jit(solution)/shard_map/ppermute | solution.py:308
  50.4 7.8 %collective-permute-start.13 = (f32[2,784,256]{2,1,0:T(8,128)S(1)}, f32[2,784,256]{2,1,0:T(8,128)S(1)}, u32[]{:S(2)}, u32[]{:S(2)}) collective-permute-start(f32[2,784,256]{2,1,0:T(8,128)S(1)} %collective-permute-done.2.refs_3_.refs_11_), channel_id=1, source_target_pairs={{0,1},{1,0},{2,3},{3,2},{4,5},{5,4},{6,7},{7,6},{8,9},{9,8},{10,11... | collective-permute-start | bytes 4816904 | tf_op jit(solution)/shard_map/ppermute | solution.py:308
  50.5 40.3 %collective-permute-start.10 = (f32[2,784,256]{2,1,0:T(8,128)}, f32[2,784,256]{2,1,0:T(8,128)}, u32[]{:S(2)}, u32[]{:S(2)}) collective-permute-start(f32[2,784,256]{2,1,0:T(8,128)} %collective-permute-done.refs_9_), channel_id=1, source_target_pairs={{0,2},{1,3},{2,4},{3,5},{4,6},{5,7},{6,0},{7,1},{8,10},{9,11},{10,... | collective-permute-start | bytes 4816904 | tf_op jit(solution)/shard_map/ppermute | solution.py:308
  50.5 40.3 %collective-permute-start.9 = (f32[2,784,256]{2,1,0:T(8,128)S(1)}, f32[2,784,256]{2,1,0:T(8,128)}, u32[]{:S(2)}, u32[]{:S(2)}) collective-permute-start(f32[2,784,256]{2,1,0:T(8,128)S(1)} %collective-permute-done.2.refs_3_.refs_11_), channel_id=1, source_target_pairs={{0,6},{1,7},{2,0},{3,1},{4,2},{5,3},{6,4},{7,5},{8,14},{9,15},{10,... | collective-permute-start | bytes 4816904 | tf_op jit(solution)/shard_map/ppermute | solution.py:308
  59.4 31.1 %collective-permute-start.14 = (f32[32,256]{1,0:T(8,128)S(1)}, f32[32,256]{1,0:T(8,128)S(1)}, u32[]{:S(2)}, u32[]{:S(2)}) collective-permute-start(f32[32,256]{1,0:T(8,128)S(1)} %add.53), channel_id=1, source_target_pairs={{0,2},{1,3},{2,4},{3,5},{4,6},{5,7},{6,0},{7,1},{8,10},{9,11},{10,... | collective-permute-start | bytes 98312 | tf_op jit(solution)/shard_map/ppermute | solution.py:308
  59.9 30.9 %collective-permute-start.15 = (f32[32,256]{1,0:T(8,128)S(1)}, f32[32,256]{1,0:T(8,128)S(1)}, u32[]{:S(2)}, u32[]{:S(2)}) collective-permute-start(f32[32,256]{1,0:T(8,128)S(1)} %add.53), channel_id=1, source_target_pairs={{0,4},{1,5},{2,6},{3,7},{4,0},{5,1},{6,2},{7,3},{8,12},{9,13},{10,... | collective-permute-start | bytes 98312 | tf_op jit(solution)/shard_map/ppermute | solution.py:308
  62.6 28.2 %collective-permute-start.16 = (f32[32,256]{1,0:T(8,128)S(1)}, f32[32,256]{1,0:T(8,128)S(1)}, u32[]{:S(2)}, u32[]{:S(2)}) collective-permute-start(f32[32,256]{1,0:T(8,128)S(1)} %add.53), channel_id=1, source_target_pairs={{0,6},{1,7},{2,0},{3,1},{4,2},{5,3},{6,4},{7,5},{8,14},{9,15},{10,... | collective-permute-start | bytes 98312 | tf_op jit(solution)/shard_map/ppermute | solution.py:308
  90.8 5.9 %collective-permute-start.18 = (f32[2,784,256]{2,1,0:T(8,128)}, f32[2,784,256]{2,1,0:T(8,128)}, u32[]{:S(2)}, u32[]{:S(2)}) collective-permute-start(f32[2,784,256]{2,1,0:T(8,128)} %collective-permute-done.9.refs_5_.refs_13_), channel_id=1, source_target_pairs={{0,1},{1,0},{2,3},{3,2},{4,5},{5,4},{6,7},{7,6},{8,9},{9,8},{10,11... | collective-permute-start | bytes 4816904 | tf_op jit(solution)/shard_map/ppermute | solution.py:308
  90.9 6.1 %collective-permute-start.19 = (f32[2,784,256]{2,1,0:T(8,128)}, f32[2,784,256]{2,1,0:T(8,128)}, u32[]{:S(2)}, u32[]{:S(2)}) collective-permute-start(f32[2,784,256]{2,1,0:T(8,128)} %collective-permute-done.10.refs_7_), channel_id=1, source_target_pairs={{0,1},{1,0},{2,3},{3,2},{4,5},{5,4},{6,7},{7,6},{8,9},{9,8},{10,11... | collective-permute-start | bytes 4816904 | tf_op jit(solution)/shard_map/ppermute | solution.py:308
  91.4 40.6 %collective-permute-start.20 = (f32[2,784,256]{2,1,0:T(8,128)}, f32[2,784,256]{2,1,0:T(8,128)}, u32[]{:S(2)}, u32[]{:S(2)}) collective-permute-start(f32[2,784,256]{2,1,0:T(8,128)} %collective-permute-done.9.refs_5_.refs_13_), channel_id=1, source_target_pairs={{0,6},{1,7},{2,0},{3,1},{4,2},{5,3},{6,4},{7,5},{8,14},{9,15},{10,... | collective-permute-start | bytes 4816904 | tf_op jit(solution)/shard_map/ppermute | solution.py:308
  94.2 38.1 %collective-permute-start.21 = (f32[2,784,256]{2,1,0:T(8,128)S(1)}, f32[2,784,256]{2,1,0:T(8,128)}, u32[]{:S(2)}, u32[]{:S(2)}) collective-permute-start(f32[2,784,256]{2,1,0:T(8,128)S(1)} %collective-permute-done.2.refs_3_.refs_11_), channel_id=1, source_target_pairs={{0,2},{1,3},{2,4},{3,5},{4,6},{5,7},{6,0},{7,1},{8,10},{9,11},{10,... | collective-permute-start | bytes 4816904 | tf_op jit(solution)/shard_map/ppermute | solution.py:308
  94.2 2.5 %collective-permute-start.17 = (f32[32,256]{1,0:T(8,128)S(1)}, f32[32,256]{1,0:T(8,128)S(1)}, u32[]{:S(2)}, u32[]{:S(2)}) collective-permute-start(f32[32,256]{1,0:T(8,128)S(1)} %add_add_fusion.1), channel_id=1, source_target_pairs={{0,1},{1,0},{2,3},{3,2},{4,5},{5,4},{6,7},{7,6},{8,9},{9,8},{10,11... | collective-permute-start | bytes 98312 | tf_op jit(solution)/shard_map/ppermute | solution.py:308
  94.3 37.7 %copy-start.10 = (s32[6]{0:T(128)}, s32[6]{0:T(128)S(1)}, u32[]{:S(2)}) copy-start(s32[6]{0:T(128)S(1)} %stack.43.refs_0_) | copy-start | bytes 76
  132.3 8.6 %collective-permute-start.22 = (f32[2,784,256]{2,1,0:T(8,128)}, f32[2,784,256]{2,1,0:T(8,128)}, u32[]{:S(2)}, u32[]{:S(2)}) collective-permute-start(f32[2,784,256]{2,1,0:T(8,128)} %collective-permute-done.20.refs_7_.refs_15_), channel_id=1, source_target_pairs={{0,1},{1,0},{2,3},{3,2},{4,5},{5,4},{6,7},{7,6},{8,9},{9,8},{10,11... | collective-permute-start | bytes 4816904 | tf_op jit(solution)/shard_map/ppermute | solution.py:308
  132.3 8.6 %collective-permute-start.23 = (f32[2,784,256]{2,1,0:T(8,128)}, f32[2,784,256]{2,1,0:T(8,128)}, u32[]{:S(2)}, u32[]{:S(2)}) collective-permute-start(f32[2,784,256]{2,1,0:T(8,128)} %collective-permute-done.21.refs_9_.refs_17_), channel_id=1, source_target_pairs={{0,1},{1,0},{2,3},{3,2},{4,5},{5,4},{6,7},{7,6},{8,9},{9,8},{10,11... | collective-permute-start | bytes 4816904 | tf_op jit(solution)/shard_map/ppermute | solution.py:308
  133.7 18.4 %all-to-all-start.2 = ((f32[8,64,256]{2,1,0:T(8,128)}), f32[8,64,256]{2,1,0:T(8,128)}, u32[]{:S(2)}, u32[]{:S(2)}) async-start(f32[8,64,256]{2,1,0:T(8,128)} %broadcast_in_dim.10), calls=%async_computation.2 | async-start | bytes 1048576 | tf_op jit(solution)/shard_map/all_to_all | solution.py:371
  152.0 15.2 %all-to-all-start.1 = ((f32[8,16,512]{2,1,0:T(8,128)}), f32[8,16,512]{2,1,0:T(8,128)S(1)}, u32[]{:S(2)}, u32[]{:S(2)}) async-start(f32[8,16,512]{2,1,0:T(8,128)} %bitcast.17), calls=%async_computation.1 | async-start | bytes 524288 | tf_op jit(solution)/shard_map/all_to_all | solution.py:375
  170.6 12.1 %all-to-all-start.3 = ((f32[8,16,512]{2,1,0:T(8,128)}), f32[8,16,512]{2,1,0:T(8,128)S(1)}, u32[]{:S(2)}, u32[]{:S(2)}) async-start(f32[8,16,512]{2,1,0:T(8,128)} %shard_map.60), calls=%async_computation.3 | async-start | bytes 524288 | tf_op jit(solution)/shard_map/all_to_all | solution.py:377
  (13 other events, 41.9 us)
where the time goes:
time: 204 us; the launch traced here: 201 us
  waiting for transfers between devices  82.4 us (40%)
  Pallas kernels  51.5 us (25%)
  starting transfers between devices  47 us (23%)
  local copies, waits for them, and re-layouts  18.9 us (9%)
    ppermute x21, waiting for transfers between devices, along_col(): return lax.ppermute(value, 'col', [(c, to(c)) for c in range(grid_cols)])  41.2 us
    all_to_all x1, waiting for transfers between devices, shards(): lax.all_to_all(dealt, 'row', 0, 0, tiled=True)  24.6 us
    pallas_call x2, Pallas kernels, inner(): pl.pallas_call(lambda *refs: inner_kernel(*refs, count=count, grid_rows=g...  18.5 us
    ppermute x21, starting transfers between devices, along_col(): return lax.ppermute(value, 'col', [(c, to(c)) for c in range(grid_cols)])  17.6 us
    pallas_call x1, Pallas kernels, apply(): pl.pallas_call(lambda *refs: apply_kernel(*refs, count=count, grid_rows=g...  17.5 us
    ppermute x3, waiting for transfers between devices, along_row(): return lax.ppermute(value, 'row', [(r, to(r)) for r in range(grid_rows)])  10.6 us
    unnamed x34, local copies, waits for them, and re-layouts  9.85 us
    pallas_call x1, Pallas kernels, deal(): pl.pallas_call(lambda i, o: deal_kernel(i, o, pairs=local // 128 // steps...  8.88 us
  transfers between devices with their start and end apart: 28, of which 15 were waited for; matrix products, arithmetic and copies ran while one was open for 5% of the time, Pallas kernels for 16%

commit v1 on v0

--- a/solution.py
+++ b/solution.py
@@ -126,78 +126,159 @@
     )(info, panels)
 
 
-def inner_kernel(info, v_ref, w_ref, *refs, count, grid_rows, chunk):
-    *r_refs, o_ref, held, sems = refs
+def inner_kernel(info, v_ref, w_ref, *refs, count, parts, grid_rows, chunk):
+    r_refs, refs = refs[:count], refs[count:]
+    o_refs, (high_ref, low_ref, held, v_held, total, sems, v_sems) = refs[:parts], refs[parts:]
     narrow = v_ref.shape[0]
-    panels, total, width = held.shape
+    panels, depth, width = held.shape
     sources = ring_sources(r_refs, info)
-    base = info[3] * total
-    for block, views in sources:
+    base = info[3] * depth
+
+    def v_copy(q):
+        from_at = pl.ds(pl.multiple_of(base + q * chunk, 128), chunk)
+        to_at = pl.ds(pl.multiple_of(q * chunk, 128), chunk)
+        return pltpu.make_async_copy(v_ref.at[:, from_at], v_held.at[:, to_at], v_sems.at[q])
+
+    for turn_at, (block, views) in enumerate(sources):
+        if turn_at < count - 1:
+            v_copy(lax.rem(2 * info[4] + turn_at, count - 1)).start()
         start_block(info, views, held, sems, block, base, grid_rows)
-    o_ref[...] = w_ref[...]
+    total[...] = w_ref[...]
     view = sources[0][1][0]
-    wait_block(info, view, held, sems, 0, base, grid_rows)
-
-    def step(q, carry):
-        wait_block(info, view, held, sems, q + 1, base, grid_rows)
+    begin = 2 * info[4]
+
+    def step(done, carry):
+        turn_at, k = done // panels, lax.rem(done, panels)
+        q = lax.rem(begin + turn_at, count - 1)
         at = pl.multiple_of(q * chunk, chunk)
         first = base + at
-        for k in range(panels):
-
-            def work(block, k=k):
-                high, low = split(block)
-                v_high, v_low = split(v_ref[:, pl.ds(pl.multiple_of(first, 128), chunk)])
-                both = jnp.concatenate([v_high, v_low], axis=0)
-                main = jnp.dot(both, high, preferred_element_type=F32)
-                rest = jnp.dot(v_high, low, preferred_element_type=F32)
-                o_ref[:, k * width : (k + 1) * width] += main[:narrow] + (main[narrow:] + rest)
-
-            each_case(info, k, first, chunk, width, grid_rows, lambda k=k: held[k, pl.ds(at, chunk), :], work)
+        across = pl.ds(pl.multiple_of(k * width, width), width)
+
+        pl.when(k == 0)(v_copy(q).wait)
+
+        @pl.when((k == 0) & ((q == 0) | (turn_at == 0)))
+        def _():
+            wait_block(info, view, held, sems, q, base, grid_rows)
+
+        @pl.when((k == 0) & (q + 1 != begin))
+        def _():
+            wait_block(info, view, held, sems, q + 1, base, grid_rows)
+
+        def work(block):
+            high, low = split(block)
+            high_ref[pl.ds(at, chunk), across] = high
+            low_ref[pl.ds(at, chunk), across] = low
+            v_high, v_low = split(v_held[:, pl.ds(pl.multiple_of(q * chunk, 128), chunk)])
+            both = jnp.concatenate([v_high, v_low], axis=0)
+            main = jnp.dot(both, high, preferred_element_type=F32)
+            rest = jnp.dot(v_high, low, preferred_element_type=F32)
+            total[:, across] += main[:narrow] + (main[narrow:] + rest)
+
+        each_case(info, k, first, chunk, width, grid_rows, lambda: held[k, pl.ds(at, chunk), :], work)
         return carry
 
-    lax.fori_loop(0, count - 1, step, 0)
-
-
-def inner(info, v, start, gathered, count, shape, grid_rows):
+    lax.fori_loop(0, (count - 1) * panels, step, 0)
+    size = narrow // parts
+    for part, o_ref in enumerate(o_refs):
+        at = lax.rem(info[6] + part, parts) * size
+        o_ref[...] = total[pl.ds(pl.multiple_of(at, size), size), :]
+
+
+def inner(info, v, start, gathered, parts, shape, grid_rows):
     panels, rows, width = shape
     narrow = v.shape[0]
+    count = len(gathered)
     total = count * rows
     vmem = pl.BlockSpec(memory_space=pltpu.VMEM)
-    return pl.pallas_call(
-        lambda *refs: inner_kernel(*refs, count=count, grid_rows=grid_rows, chunk=total // (count - 1)),
-        in_specs=[pl.BlockSpec(memory_space=pltpu.SMEM), vmem, vmem]
-        + [pl.BlockSpec(memory_space=pltpu.HBM)] * len(gathered),
-        out_specs=vmem,
-        out_shape=jax.ShapeDtypeStruct((narrow, panels * width), F32),
+    *sums, high, low = pl.pallas_call(
+        lambda *refs: inner_kernel(
+            *refs, count=count, parts=parts, grid_rows=grid_rows, chunk=total // (count - 1)
+        ),
+        in_specs=[pl.BlockSpec(memory_space=pltpu.SMEM), pl.BlockSpec(memory_space=pltpu.HBM), vmem]
+        + [pl.BlockSpec(memory_space=pltpu.HBM)] * count,
+        out_specs=[vmem] * (parts + 2),
+        out_shape=[jax.ShapeDtypeStruct((narrow // parts, panels * width), F32)] * parts
+        + [jax.ShapeDtypeStruct((total, panels * width), BF16)] * 2,
         scratch_shapes=[
             pltpu.VMEM((panels, total, width), F32),
+            pltpu.VMEM((narrow, total), F32),
+            pltpu.VMEM((narrow, panels * width), F32),
             pltpu.SemaphoreType.DMA((panels, count)),
+            pltpu.SemaphoreType.DMA((count - 1,)),
         ],
-        compiler_params=pltpu.CompilerParams(vmem_limit_bytes=50 * 1024 * 1024),
+        compiler_params=pltpu.CompilerParams(vmem_limit_bytes=22 * 1024 * 1024),
         cost_estimate=pl.CostEstimate(
             flops=6 * narrow * panels * total * width, bytes_accessed=4 * panels * total * width, transcendentals=0
         ),
     )(info, v, start, *gathered)
-
-
-def solve_kernel(parts_ref, mix_ref, out_ref):
-    total = parts_ref[0]
-    for i in range(1, parts_ref.shape[0]):
-        total += parts_ref[i]
-    solved = jnp.dot(total, mix_ref[...], precision=lax.Precision.HIGHEST, preferred_element_type=F32)
-    for i in range(parts_ref.shape[0]):
-        out_ref[i] = solved
-
-
-def solve(parts, mix):
-    return pl.pallas_call(
-        solve_kernel, out_shape=jax.ShapeDtypeStruct(parts.shape, F32)
-    )(parts, mix)
-
-
-def mixing_kernel(upper_ref, scales_ref, gram_ref, o_ref):
-    width = scales_ref.shape[1]
-    gram = (gram_ref[:4] + gram_ref[4:]).reshape(width, width)
+    return sums, (high, low)
+
+
+def add_kernel(*refs):
+    *parts, o_ref = refs
+    total = parts[0][...]
+    for part in parts[1:]:
+        total += part[...]
+    o_ref[...] = total
+
+
+def add(*parts):
+    return pl.pallas_call(
+        add_kernel,
+        out_shape=jax.ShapeDtypeStruct(parts[0].shape, F32),
+        compiler_params=pltpu.CompilerParams(vmem_limit_bytes=2 * 1024 * 1024),
+    )(*parts)
+
+
+def solve_kernel(mine_ref, given_ref, mix_ref, out_ref):
+    out_ref[...] = exact_dot(mine_ref[...] + given_ref[...], mix_ref[...])
+
+
+def solve(mine, given, mix):
+    return pl.pallas_call(
+        solve_kernel,
+        out_shape=jax.ShapeDtypeStruct(mine.shape, F32),
+        compiler_params=pltpu.CompilerParams(vmem_limit_bytes=4 * 1024 * 1024),
+    )(mine, given, mix)
+
+
+def turn_kernel(v_ref, o_ref, held, sems, *, chunk):
+    steps = o_ref.shape[0] // chunk
+
+    def copy(q):
+        at = pl.ds(pl.multiple_of(q * chunk, chunk), chunk)
+        return pltpu.make_async_copy(v_ref.at[:, at], held.at[:, at], sems.at[q])
+
+    for q in range(steps):
+        copy(q).start()
+
+    def step(q, carry):
+        copy(q).wait()
+        at = pl.ds(pl.multiple_of(q * chunk, chunk), chunk)
+        o_ref[at, :] = held[:, at].T
+        return carry
+
+    lax.fori_loop(0, steps, step, 0)
+
+
+def turn(v, chunk):
+    return pl.pallas_call(
+        lambda *refs: turn_kernel(*refs, chunk=chunk),
+        in_specs=[pl.BlockSpec(memory_space=pltpu.HBM)],
+        out_specs=pl.BlockSpec(memory_space=pltpu.VMEM),
+        out_shape=jax.ShapeDtypeStruct(v.shape[::-1], F32),
+        scratch_shapes=[pltpu.VMEM(v.shape, F32), pltpu.SemaphoreType.DMA((v.shape[1] // chunk,))],
+        compiler_params=pltpu.CompilerParams(vmem_limit_bytes=9 * 1024 * 1024),
+    )(v)
+
+
+def mixing_kernel(info, upper_ref, scales_ref, *refs):
+    *part_refs, o_ref, gram = refs
+    width = gram.shape[0]
+    part = width // len(part_refs)
+    for step, part_ref in enumerate(part_refs):
+        at = lax.rem(info[6] + len(part_refs) - step, len(part_refs)) * part
+        gram[pl.ds(pl.multiple_of(at, part), part), :] = part_ref[...]
     row = lax.broadcasted_iota(jnp.int32, (width, width), 0)
     column = lax.broadcasted_iota(jnp.int32, (width, width), 1)
 
@@ -206,94 +287,97 @@
         return jnp.where(row < column, upper_ref[k], diagonal)
 
     zero, one = factor(0), factor(1)
-    corner = exact_dot(one, exact_dot(gram, zero))
+    corner = exact_dot(one, exact_dot(gram[...], zero))
     o_ref[:width, :width] = zero.T
     o_ref[:width, width:] = -corner.T
     o_ref[width:, :width] = jnp.zeros((width, width), F32)
     o_ref[width:, width:] = one.T
 
 
-def mixing(factor_upper, scales, gram):
+def mixing(info, factor_upper, scales, parts):
     panels, width = scales.shape
+    vmem = pl.BlockSpec(memory_space=pltpu.VMEM)
     return pl.pallas_call(
         mixing_kernel,
+        in_specs=[pl.BlockSpec(memory_space=pltpu.SMEM)] + [vmem] * (2 + len(parts)),
+        out_specs=vmem,
         out_shape=jax.ShapeDtypeStruct((panels * width, panels * width), F32),
-        compiler_params=pltpu.CompilerParams(vmem_limit_bytes=16 * 1024 * 1024),
-    )(factor_upper, scales, gram)
-
-
-def apply_kernel(info, v_ref, t_ref, *refs, count, grid_rows):
-    *r_refs, o_ref, t_scr, held, moving, sems, v_sems, o_sems = refs
-    panels, total, width = held.shape
-    narrow = t_ref.shape[0]
-    rows = total // (2 * count)
-    sources = [(info[3] * count + block, views) for block, views in ring_sources(r_refs[:count], info)]
-    sources += [((1 - info[3]) * count + block, views) for block, views in ring_sources(r_refs[count:], info)]
-
-    def place(block):
-        return pl.ds(pl.multiple_of(block * rows, rows), rows)
-
-    def v_copy(block):
-        return pltpu.make_async_copy(v_ref.at[place(block)], moving.at[place(block)], v_sems.at[block])
-
-    def o_copy(block):
-        return pltpu.make_async_copy(moving.at[place(block)], o_ref.at[place(block)], o_sems.at[block])
-
-    for block, views in sources:
-        v_copy(block).start()
-        start_block(info, views, held, sems, block, 0, grid_rows)
+        scratch_shapes=[pltpu.VMEM((width, width), F32)],
+        compiler_params=pltpu.CompilerParams(vmem_limit_bytes=8 * 1024 * 1024),
+    )(info, factor_upper, scales, *parts)
+
+
+def apply_kernel(info, v_ref, *refs, parts, chunk, grid_rows):
+    t_refs, refs = refs[:parts], refs[parts:]
+    halves, (o_ref, t_all, t_scr, held, sems) = refs[:4], refs[4:]
+    total, depth = halves[0].shape
+    panels, width, _ = t_scr.shape
+    size = t_refs[0].shape[0]
+    narrow = size * parts
+    for part, t_ref in enumerate(t_refs):
+        at = lax.rem(info[6] + parts - part, parts) * size
+        t_all[pl.ds(pl.multiple_of(at, size), size), :] = t_ref[...]
     for k in range(panels):
-        high, low = split(t_ref[:, k * width : (k + 1) * width].T)
+        high, low = split(t_all[:, k * width : (k + 1) * width].T)
         t_scr[k, :, :narrow] = high
         t_scr[k, :, narrow:] = low
-
-    def step(done, carry):
-        half = jnp.where(done < count, info[3], 1 - info[3])
-        block = half * count + ring_block(info, lax.rem(done, count))
-        first = block * rows
-        v_copy(block).wait()
-        wait_block(info, sources[0][1][0], held, sems, block, 0, grid_rows)
-        for k in range(panels):
-
-            def work(value, k=k):
-                high, low = split(value)
-                main = jnp.dot(high, t_scr[k], preferred_element_type=F32)
-                rest = jnp.dot(low, t_scr[k, :, :narrow], preferred_element_type=F32)
-                moving[place(block), :] -= main[:, :narrow] + (main[:, narrow:] + rest)
-
-            each_case(info, k, first, rows, width, grid_rows, lambda k=k: held[k, place(block), :], work)
-        o_copy(block).start()
-        return carry
-
-    lax.fori_loop(0, 2 * count, step, 0)
-    for block in range(2 * count):
-        o_copy(block).wait()
-
-
-def apply(info, v, t, gathered, count, shape, grid_rows):
-    panels, rows, width = shape
+    steps, slots = total // chunk, held.shape[0]
+
+    def copy_of(slot, first):
+        return pltpu.make_async_copy(held.at[slot], o_ref.at[pl.ds(first, chunk), :], sems.at[slot])
+
+    for half, (high_ref, low_ref) in enumerate((halves[:2], halves[2:])):
+        side = info[3] if half == 0 else 1 - info[3]
+
+        def step(q, carry, half=half, side=side, high_ref=high_ref, low_ref=low_ref):
+            at = pl.multiple_of(q * chunk, chunk)
+            first = pl.multiple_of(side * total + at, chunk)
+            done = half * steps + q
+            slot = lax.rem(done, slots)
+            pl.when(done >= slots)(copy_of(slot, first).wait)
+            held[slot] = v_ref[pl.ds(first, chunk), :]
+            last = global_row(first + chunk - 1, info[2], grid_rows)
+
+            def panel(k, carry):
+                across = pl.ds(pl.multiple_of(k * width, width), width)
+
+                @pl.when(last >= info[k])
+                def _():
+                    main = jnp.dot(high_ref[pl.ds(at, chunk), across], t_scr[k], preferred_element_type=F32)
+                    rest = jnp.dot(
+                        low_ref[pl.ds(at, chunk), across], t_scr[k, :, :narrow], preferred_element_type=F32
+                    )
+                    held[slot] -= main[:, :narrow] + (main[:, narrow:] + rest)
+
+                return carry
+
+            lax.fori_loop(0, panels, panel, 0)
+            copy_of(slot, first).start()
+            return carry
+
+        lax.fori_loop(0, steps, step, 0)
+    for slot in range(slots):
+        copy_of(slot, 0).wait()
+
+
+def apply(info, v, t, own, other, chunk, grid_rows):
     narrow = v.shape[1]
-    total = 2 * count * rows
-    anywhere = pl.BlockSpec(memory_space=pltpu.HBM)
-    return pl.pallas_call(
-        lambda *refs: apply_kernel(*refs, count=count, grid_rows=grid_rows),
-        in_specs=[pl.BlockSpec(memory_space=pltpu.SMEM), anywhere, pl.BlockSpec(memory_space=pltpu.VMEM)]
-        + [anywhere] * len(gathered),
-        out_specs=anywhere,
+    depth = t[0].shape[1]
+    slots = 7
+    vmem = pl.BlockSpec(memory_space=pltpu.VMEM)
+    return pl.pallas_call(
+        lambda *refs: apply_kernel(*refs, parts=len(t), chunk=chunk, grid_rows=grid_rows),
+        in_specs=[pl.BlockSpec(memory_space=pltpu.SMEM)] + [vmem] * (5 + len(t)),
+        out_specs=pl.BlockSpec(memory_space=pltpu.HBM),
         out_shape=jax.ShapeDtypeStruct(v.shape, F32),
         scratch_shapes=[
-            pltpu.VMEM((panels, width, 2 * narrow), BF16),
-            pltpu.VMEM((panels, total, width), F32),
-            pltpu.VMEM((total, narrow), F32),
-            pltpu.SemaphoreType.DMA((panels, 2 * count)),
-            pltpu.SemaphoreType.DMA((2 * count,)),
-            pltpu.SemaphoreType.DMA((2 * count,)),
+            pltpu.VMEM((narrow, depth), F32),
+            pltpu.VMEM((2, depth // 2, 2 * narrow), BF16),
+            pltpu.VMEM((slots, chunk, narrow), F32),
+            pltpu.SemaphoreType.DMA((slots,)),
         ],
-        compiler_params=pltpu.CompilerParams(vmem_limit_bytes=56 * 1024 * 1024),
-        cost_estimate=pl.CostEstimate(
-            flops=6 * narrow * panels * total * width, bytes_accessed=4 * panels * total * width, transcendentals=0
-        ),
-    )(info, v, t, *gathered)
+        compiler_params=pltpu.CompilerParams(vmem_limit_bytes=10 * 1024 * 1024),
+    )(info, v, *t, *own, *other)
 
 
 def shards(vectors, panels, offsets, factor_upper, scales):
@@ -357,25 +441,32 @@
     other_above_across, far_across = across(other_above), across(far)
     given = across(gram)
     gram = jnp.where(core == 0, jnp.concatenate([gram, given]), jnp.concatenate([given, gram]))
-    moved, gram, other_above_across, far_across = lax.optimization_barrier(
-        (moved, gram, other_above_across, far_across)
+    gram = gram + along_row(gram, lambda r: r ^ 4)
+    own_info, other_info = info(side, ring, core, level), info(1 - side, ring, core, level)
+    moved, gram, other_above_across, far_across, own_info, other_info = lax.optimization_barrier(
+        (moved, gram, other_above_across, far_across, own_info, other_info)
     )
 
+    moved = pltpu.with_memory_space_constraint(moved, pltpu.HBM)
+
+    chunk = half * rows // (half - 1)
     own = [panels, panels_across, above, above_across, far, far_across, below, below_across]
+    own = [pltpu.with_memory_space_constraint(part, pltpu.HBM) for part in own]
     start = jnp.zeros((grid_rows * narrow, 2 * width), F32)
-    sums = inner(info(side, ring, core), moved, start, own, half, panels.shape, grid_rows)
-    sums, gram, other_far, other_below = lax.optimization_barrier((sums, gram, other_far, other_below))
-    other = [near, near_across, other_above, other_above_across]
-    other += [other_far, across(other_far), other_below, across(other_below)]
-    gram = jnp.broadcast_to(gram[None], (grid_rows,) + gram.shape)
-    gram = lax.all_to_all(gram, "row", 0, 0, tiled=True)
-    mix = mixing(factor_upper, scales, gram)
-
-    sums = inner(info(1 - side, ring, core), moved, sums, other, half, panels.shape, grid_rows)
-    parts = lax.all_to_all(sums.reshape(grid_rows, narrow, 2 * width), "row", 0, 0, tiled=True)
-    solved = solve(parts, mix)
-    solved = lax.all_to_all(solved, "row", 0, 0, tiled=True).reshape(grid_rows * narrow, 2 * width)
-    return apply(info(side, ring, core), moved.T, solved, own + other, half, panels.shape, grid_rows)
+    grams = [gram] + [along_row(gram, shifted(step)) for step in (1, 2, 3)]
+    sums, own = inner(own_info, moved, start, own, 1, panels.shape, grid_rows)
+    sums, other_far, other_below, *grams = lax.optimization_barrier((*sums, other_far, other_below, *grams))
+    other = [near, near_across, other_above, other_above_across, other_far, other_below]
+    other = [pltpu.with_memory_space_constraint(part, pltpu.HBM) for part in other]
+    other[5:] = [across(other_far), other[5], across(other_below)]
+    sums, current = lax.optimization_barrier((sums, turn(moved, 896)))
+    (mine, *sums), other = inner(other_info, moved, sums, other, 4, panels.shape, grid_rows)
+
+    mine = add(mine, *[along_row(sums[step - 1], shifted(step)) for step in (1, 2, 3)])
+    mix = mixing(own_info, factor_upper, scales, grams)
+    solved = solve(mine, along_row(mine, lambda r: r ^ 4), mix)
+    solved = [solved] + [along_row(solved, shifted(step)) for step in (1, 2, 3)]
+    return apply(own_info, current, solved, own, other, chunk, grid_rows)
 
 
 def solution(mesh):

time: 204 us -> 177 us (0.87); the launches traced: 201 us -> 177 us
  local copies, waits for them, and re-layouts: 18.9 us -> 2.95 us
  Pallas kernels: 51.5 us -> 37.6 us
  waiting for transfers between devices: 82.4 us -> 86.1 us
    ppermute x3 -> x14, waiting for transfers between devices: 10.6 us -> 40.9 us  [along_row(): return lax.ppermute(value, 'row', [(r, to(r)) for r in range(grid_rows)])]
    all_to_all x1, waiting for transfers between devices: 24.6 us -> 0.01 us  [shards(): lax.all_to_all(dealt, 'row', 0, 0, tiled=True)]
    ppermute x3 -> x14, starting transfers between devices: 5.3 us -> 26.8 us  [along_row(): return lax.ppermute(value, 'row', [(r, to(r)) for r in range(grid_rows)])]
    all_to_all x3 -> x0, starting transfers between devices: 17 us -> none  [the longest x1 7.19 us: shards(): gram = lax.all_to_all(gram, 'row', 0, 0, tiled=True)]
    pallas_call x5 -> x7, Pallas kernels: 40.8 us -> 26.9 us  [the longest x2 12.8 us: inner(): pl.pallas_call(lambda *refs: inner_kernel(*refs, count=count, parts=parts...]
    optimization_barrier x1 -> x0, local copies, waits for them, and re-layouts: 8.02 us -> none  [shards(): lax.optimization_barrier((moved, gram, other_above_across, far_across))]
    unnamed x34 -> x20, local copies, waits for them, and re-layouts: 9.85 us -> 2.76 us
    all_to_all x3 -> x0, waiting for transfers between devices: 5.98 us -> none  [the longest x1 4.52 us: shards(): lax.all_to_all(sums.reshape(grid_rows, narrow, 2 * width), 'row', 0, 0, t...]
  transfers between devices with their start and end apart: 28 -> 36, of which waited for: 15 -> 20; matrix products, arithmetic and copies ran while one was open for 5% -> 1% of each run, Pallas kernels for 16% -> 12%
where the time goes in v1:
time: 177 us
  waiting for transfers between devices  86.1 us (49%)
  starting transfers between devices  48.8 us (28%)
  Pallas kernels  37.6 us (21%)
  local copies, waits for them, and re-layouts  2.95 us (2%)
    ppermute x21, waiting for transfers between devices, along_col(): return lax.ppermute(value, 'col', [(c, to(c)) for c in range(grid_cols)])  45.2 us
    ppermute x14, waiting for transfers between devices, along_row(): return lax.ppermute(value, 'row', [(r, to(r)) for r in range(grid_rows)])  40.9 us
    ppermute x14, starting transfers between devices, along_row(): return lax.ppermute(value, 'row', [(r, to(r)) for r in range(grid_rows)])  26.8 us
    ppermute x21, starting transfers between devices, along_col(): return lax.ppermute(value, 'col', [(c, to(c)) for c in range(grid_cols)])  15 us
    pallas_call x2, Pallas kernels, inner(): pl.pallas_call(lambda *refs: inner_kernel(*refs, count=count, parts=parts...  12.8 us
    pallas_call x1, Pallas kernels, deal(): pl.pallas_call(lambda i, o: deal_kernel(i, o, pairs=local // 128 // steps...  8.88 us
    pallas_call x1, Pallas kernels, apply(): pl.pallas_call(lambda *refs: apply_kernel(*refs, parts=len(t), chunk=chun...  7.68 us
    all_to_all x1, starting transfers between devices, shards(): lax.all_to_all(dealt, 'row', 0, 0, tiled=True)  6.94 us
  transfers between devices with their start and end apart: 36, of which 20 were waited for; matrix products, arithmetic and copies ran while one was open for 1% of the time, Pallas kernels for 12%

profile of v1, /device:TPU:0, one launch (start us, length us, event | category | flops | bytes accessed | tf_op | source)
XLA Modules:
  0.0 176.7 jit_solution(2800360424178074800)
XLA Ops:
  0.0 2.0 %collective-permute-start = (f32[2,784,256]{2,1,0:T(8,128)}, f32[2,784,256]{2,1,0:T(8,128)S(1)}, u32[]{:S(2)}, u32[]{:S(2)}) collective-permute-start(f32[2,784,256]{2,1,0:T(8,128)} %refs_3_.1), channel_id=1, source_target_pairs={{0,2},{1,3},{2,4},{3,5},{4,6},{5,7},{6,0},{7,1},{8,10},{9,11},{10,... | collective-permute-start | bytes 4816904 | tf_op jit(solution)/shard_map/ppermute | solution.py:392
  2.0 2.1 %collective-permute-start.1 = (f32[2,784,256]{2,1,0:T(8,128)}, f32[2,784,256]{2,1,0:T(8,128)}, u32[]{:S(2)}, u32[]{:S(2)}) collective-permute-start(f32[2,784,256]{2,1,0:T(8,128)} %refs_3_.1), channel_id=1, source_target_pairs={{0,6},{1,7},{2,0},{3,1},{4,2},{5,3},{6,4},{7,5},{8,14},{9,15},{10,... | collective-permute-start | bytes 4816904 | tf_op jit(solution)/shard_map/ppermute | solution.py:392
  7.8 1.8 %shard_map.56 = (f32[64,256]{1,0:T(8,128)S(1)}, f32[64,256]{1,0:T(8,128)S(1)}, f32[64,256]{1,0:T(8,128)S(1)}, f32[64,256]{1,0:T(8,128)S(1)}) custom-call(s32[5]{0:T(128)S(1)} %pad_add_fusion.refs_0_, f32[2,784,256]{2,1,0:T(8,128)S(1)} %copy-done), custom_call_target="tpu_custom_call" | custom-call | tf_op jit(solution)/shard_map/pallas_call | solution.py:119
  9.6 3.1 %collective-permute-start.5 = (f32[64,256]{1,0:T(8,128)S(1)}, f32[64,256]{1,0:T(8,128)S(1)}, u32[]{:S(2)}, u32[]{:S(2)}) collective-permute-start(f32[64,256]{1,0:T(8,128)S(1)} %get-tuple-element.50), channel_id=1, source_target_pairs={{0,48},{16,0},{32,16},{48,32},{64,112},{80,64},{96,80},{112,96},{1... | collective-permute-start | bytes 196616 | tf_op jit(solution)/shard_map/ppermute | solution.py:395
  12.7 2.0 %collective-permute-done.5 = f32[64,256]{1,0:T(8,128)S(1)} collective-permute-done((f32[64,256]{1,0:T(8,128)S(1)}, f32[64,256]{1,0:T(8,128)S(1)}, u32[]{:S(2)}, u32[]{:S(2)}) %collective-permute-start.5) | collective-permute-done | bytes 65568 | tf_op jit(solution)/shard_map/ppermute | solution.py:395
  14.7 2.7 %collective-permute-start.4 = (f32[64,256]{1,0:T(8,128)S(1)}, f32[64,256]{1,0:T(8,128)S(1)}, u32[]{:S(2)}, u32[]{:S(2)}) collective-permute-start(f32[64,256]{1,0:T(8,128)S(1)} %get-tuple-element.49), channel_id=1, source_target_pairs={{0,32},{16,48},{32,0},{48,16},{64,96},{80,112},{96,64},{112,80},{1... | collective-permute-start | bytes 196616 | tf_op jit(solution)/shard_map/ppermute | solution.py:395
  17.3 3.1 %collective-permute-done.4 = f32[64,256]{1,0:T(8,128)S(1)} collective-permute-done((f32[64,256]{1,0:T(8,128)S(1)}, f32[64,256]{1,0:T(8,128)S(1)}, u32[]{:S(2)}, u32[]{:S(2)}) %collective-permute-start.4) | collective-permute-done | bytes 65568 | tf_op jit(solution)/shard_map/ppermute | solution.py:395
  21.5 4.9 %collective-permute-done.3 = f32[64,256]{1,0:T(8,128)S(1)} collective-permute-done((f32[64,256]{1,0:T(8,128)S(1)}, f32[64,256]{1,0:T(8,128)S(1)}, u32[]{:S(2)}, u32[]{:S(2)}) %collective-permute-start.3) | collective-permute-done | bytes 65568 | tf_op jit(solution)/shard_map/ppermute | solution.py:395
  28.3 8.9 %shard_map.55 = f32[8,16,12544]{2,1,0:T(8,128)} custom-call(f32[16,100352]{1,0:T(8,128)} %bitcast.14), custom_call_target="tpu_custom_call" | custom-call | tf_op jit(solution)/shard_map/pallas_call | solution.py:45
  37.1 4.5 %collective-permute-done.7 = f32[32,256]{1,0:T(8,128)S(1)} collective-permute-done((f32[32,256]{1,0:T(8,128)S(1)}, f32[32,256]{1,0:T(8,128)S(1)}, u32[]{:S(2)}, u32[]{:S(2)}) %collective-permute-start.7) | collective-permute-done | bytes 32800 | tf_op jit(solution)/shard_map/ppermute | solution.py:392
  41.7 6.9 %all-to-all-start = ((f32[8,16,12544]{2,1,0:T(8,128)}), f32[8,16,12544]{2,1,0:T(8,128)}, u32[]{:S(2)}, u32[]{:S(2)}) async-start(f32[8,16,12544]{2,1,0:T(8,128)} %shard_map.55), calls=%async_computation | async-start | bytes 12845056 | tf_op jit(solution)/shard_map/all_to_all | solution.py:433
  49.2 1.7 collective-permute-start.9
  51.2 2.2 %collective-permute-done.11.refs_10_ = f32[2,784,256]{2,1,0:T(8,128)S(1)} collective-permute-done((f32[2,784,256]{2,1,0:T(8,128)S(1)}, f32[2,784,256]{2,1,0:T(8,128)S(1)}, u32[]{:S(2)}, u32[]{:S(2)}) %collective-permute-start.11) | collective-permute-done | bytes 1605664 | tf_op jit(solution)/shard_map/ppermute | solution.py:392
  53.5 3.0 %collective-permute-done.12.refs_6_ = f32[2,784,256]{2,1,0:T(8,128)S(1)} collective-permute-done((f32[2,784,256]{2,1,0:T(8,128)}, f32[2,784,256]{2,1,0:T(8,128)S(1)}, u32[]{:S(2)}, u32[]{:S(2)}) %collective-permute-start.12) | collective-permute-done | bytes 1605664 | tf_op jit(solution)/shard_map/ppermute | solution.py:392
  58.0 1.7 collective-permute-start.16
  61.0 26.7 %collective-permute-done.16 = f32[32,256]{1,0:T(8,128)S(1)} collective-permute-done((f32[32,256]{1,0:T(8,128)S(1)}, f32[32,256]{1,0:T(8,128)S(1)}, u32[]{:S(2)}, u32[]{:S(2)}) %collective-permute-start.16) | collective-permute-done | bytes 32800 | tf_op jit(solution)/shard_map/ppermute | solution.py:392
  89.1 1.6 collective-permute-done.14
  91.6 1.7 collective-permute-start.22
  93.4 2.9 %collective-permute-done.17 = f32[32,256]{1,0:T(8,128)S(1)} collective-permute-done((f32[32,256]{1,0:T(8,128)S(1)}, f32[32,256]{1,0:T(8,128)S(1)}, u32[]{:S(2)}, u32[]{:S(2)}) %collective-permute-start.17) | collective-permute-done | bytes 32800 | tf_op jit(solution)/shard_map/ppermute | solution.py:392
  96.3 3.5 %collective-permute-start.18 = (f32[64,256]{1,0:T(8,128)S(1)}, f32[64,256]{1,0:T(8,128)S(1)}, u32[]{:S(2)}, u32[]{:S(2)}) collective-permute-start(f32[64,256]{1,0:T(8,128)S(1)} %maximum_select_fusion), channel_id=1, source_target_pairs={{0,64},{16,80},{32,96},{48,112},{64,0},{80,16},{96,32},{112,48},{1... | collective-permute-start | bytes 196616 | tf_op jit(solution)/shard_map/ppermute | solution.py:395
  100.0 21.6 %collective-permute-done.18 = f32[64,256]{1,0:T(8,128)S(1)} collective-permute-done((f32[64,256]{1,0:T(8,128)S(1)}, f32[64,256]{1,0:T(8,128)S(1)}, u32[]{:S(2)}, u32[]{:S(2)}) %collective-permute-start.18) | collective-permute-done | bytes 65568 | tf_op jit(solution)/shard_map/ppermute | solution.py:395
  123.2 3.0 %collective-permute-start.24 = (f32[64,256]{1,0:T(8,128)S(1)}, f32[64,256]{1,0:T(8,128)S(1)}, u32[]{:S(2)}, u32[]{:S(2)}) collective-permute-start(f32[64,256]{1,0:T(8,128)S(1)} %add.59.refs_0_), channel_id=1, source_target_pairs={{0,32},{16,48},{32,0},{48,16},{64,96},{80,112},{96,64},{112,80},{1... | collective-permute-start | bytes 196616 | tf_op jit(solution)/shard_map/ppermute | solution.py:395
  127.3 4.4 %shard_map.57 = (f32[128,512]{1,0:T(8,128)S(1)}, bf16[6272,512]{1,0:T(8,128)(2,1)S(1)}, bf16[6272,512]{1,0:T(8,128)(2,1)S(1)}) custom-call(s32[7]{0:T(128)S(1)} %stack.45.refs_0_.info, f32[128,12544]{1,0:T(8,128)} %bitcast.7.refs_1_.refs_0_, f32[128,512]{1,0:T(8,128)S(1)} %broadcast_in_dim.3.refs_2_, f32[2,784,256]{2,1,0:T(8,128)} %refs_3_.1, ...), custom_call_target="tpu_custom_call" | custom-call | flops 2466250752 | bytes 12845056 | tf_op jit(solution)/shard_map/pallas_call | solution.py:193
  132.4 4.0 %shard_map.58.refs_1_ = f32[12544,128]{1,0:T(8,128)S(1)} custom-call(f32[128,12544]{1,0:T(8,128)} %bitcast.7.refs_1_.refs_0_), custom_call_target="tpu_custom_call" | custom-call | tf_op jit(solution)/shard_map/pallas_call | solution.py:265
  137.9 8.4 %shard_map.59 = (f32[32,512]{1,0:T(8,128)S(1)}, f32[32,512]{1,0:T(8,128)S(1)}, f32[32,512]{1,0:T(8,128)S(1)}, f32[32,512]{1,0:T(8,128)S(1)}, bf16[6272,512]{1,0:...) custom-call(s32[7]{0:T(128)S(1)} %stack.47.refs_0_, f32[128,12544]{1,0:T(8,128)} %bitcast.7.refs_1_.refs_0_, ...), custom_call_target="tpu_custom_call" | custom-call | flops 2466250752 | bytes 12845056 | tf_op jit(solution)/shard_map/pallas_call | solution.py:193
  147.3 1.7 collective-permute-start.29
  150.5 2.8 %collective-permute-done.28.refs_1_ = f32[32,512]{1,0:T(8,128)S(1)} collective-permute-done((f32[32,512]{1,0:T(8,128)S(1)}, f32[32,512]{1,0:T(8,128)S(1)}, u32[]{:S(2)}, u32[]{:S(2)}) %collective-permute-start.28) | collective-permute-done | bytes 65568 | tf_op jit(solution)/shard_map/ppermute | solution.py:395
  153.9 2.5 %collective-permute-start.31 = (f32[32,512]{1,0:T(8,128)S(1)}, f32[32,512]{1,0:T(8,128)S(1)}, u32[]{:S(2)}, u32[]{:S(2)}) collective-permute-start(f32[32,512]{1,0:T(8,128)S(1)} %shard_map.60.mine_ref), channel_id=1, source_target_pairs={{0,64},{16,80},{32,96},{48,112},{64,0},{80,16},{96,32},{112,48},{1... | collective-permute-start | bytes 196616 | tf_op jit(solution)/shard_map/ppermute | solution.py:395
  156.4 1.8 %shard_map.61.mix_ref = f32[512,512]{1,0:T(8,128)S(1)} custom-call(s32[7]{0:T(128)S(1)} %stack.45.refs_0_.info, f32[2,256,256]{2,1,0:T(8,128)S(1)} %copy-done.1, f32[2,256]{1,0:T(2,128)S(1)} %copy-done.2, f32[64,256]{1,0:T(8,128)S(1)} %add.59.refs_0_, f32[64,256]{1,0:T(8,128)S(1)} %collective-permute-done.23.refs_1_, ...), custom_call_target="tpu_custom_call" | custom-call | tf_op jit(solution)/shard_map/pallas_call | solution.py:300
  161.5 3.1 %collective-permute-start.33 = (f32[32,512]{1,0:T(8,128)S(1)}, f32[32,512]{1,0:T(8,128)S(1)}, u32[]{:S(2)}, u32[]{:S(2)}) collective-permute-start(f32[32,512]{1,0:T(8,128)S(1)} %shard_map.62.refs_2_), channel_id=1, source_target_pairs={{0,32},{16,48},{32,0},{48,16},{64,96},{80,112},{96,64},{112,80},{1... | collective-permute-start | bytes 196616 | tf_op jit(solution)/shard_map/ppermute | solution.py:395
  165.9 1.6 collective-permute-done.33.refs_4_
  168.8 7.7 %shard_map.63 = f32[12544,128]{1,0:T(8,128)} custom-call(s32[7]{0:T(128)S(1)} %stack.45.refs_0_.info, f32[12544,128]{1,0:T(8,128)S(1)} %shard_map.58.refs_1_, f32[32,512]{1,0:T(8,128)S(1)} %shard_map.62.refs_2_, f32[32,512]{1,0:T(8,128)S(1)} %collective-permute-done.32.refs_3_, f32[32,512]{1,0:T(8,128)S(1)} %collective-permute-done.33.refs_4_, ...), custom_call_target="tpu_custom_call" | custom-call | tf_op jit(solution)/shard_map/pallas_call | solution.py:368
  (80 shorter events, 26.4 us)
Async XLA Ops:
  0.0 41.6 %collective-permute-start = (f32[2,784,256]{2,1,0:T(8,128)}, f32[2,784,256]{2,1,0:T(8,128)S(1)}, u32[]{:S(2)}, u32[]{:S(2)}) collective-permute-start(f32[2,784,256]{2,1,0:T(8,128)} %refs_3_.1), channel_id=1, source_target_pairs={{0,2},{1,3},{2,4},{3,5},{4,6},{5,7},{6,0},{7,1},{8,10},{9,11},{10,... | collective-permute-start | bytes 4816904 | tf_op jit(solution)/shard_map/ppermute | solution.py:392
  2.0 39.6 %collective-permute-start.1 = (f32[2,784,256]{2,1,0:T(8,128)}, f32[2,784,256]{2,1,0:T(8,128)}, u32[]{:S(2)}, u32[]{:S(2)}) collective-permute-start(f32[2,784,256]{2,1,0:T(8,128)} %refs_3_.1), channel_id=1, source_target_pairs={{0,6},{1,7},{2,0},{3,1},{4,2},{5,3},{6,4},{7,5},{8,14},{9,15},{10,... | collective-permute-start | bytes 4816904 | tf_op jit(solution)/shard_map/ppermute | solution.py:392
  4.1 37.5 %collective-permute-start.2 = (f32[2,784,256]{2,1,0:T(8,128)}, f32[2,784,256]{2,1,0:T(8,128)S(1)}, u32[]{:S(2)}, u32[]{:S(2)}) collective-permute-start(f32[2,784,256]{2,1,0:T(8,128)} %refs_3_.1), channel_id=1, source_target_pairs={{0,8},{1,9},{2,10},{3,11},{4,12},{5,13},{6,14},{7,15},{8,0},{9,1},... | collective-permute-start | bytes 4816904 | tf_op jit(solution)/shard_map/ppermute | solution.py:392
  5.6 36.0 %collective-permute-start.8 = (f32[2,784,256]{2,1,0:T(8,128)}, f32[2,784,256]{2,1,0:T(8,128)}, u32[]{:S(2)}, u32[]{:S(2)}) collective-permute-start(f32[2,784,256]{2,1,0:T(8,128)} %refs_3_.1), channel_id=1, source_target_pairs={{0,1},{1,0},{2,3},{3,2},{4,5},{5,4},{6,7},{7,6},{8,9},{9,8},{10,11... | collective-permute-start | bytes 4816904 | tf_op jit(solution)/shard_map/ppermute | solution.py:392
  9.6 5.1 %collective-permute-start.5 = (f32[64,256]{1,0:T(8,128)S(1)}, f32[64,256]{1,0:T(8,128)S(1)}, u32[]{:S(2)}, u32[]{:S(2)}) collective-permute-start(f32[64,256]{1,0:T(8,128)S(1)} %get-tuple-element.50), channel_id=1, source_target_pairs={{0,48},{16,0},{32,16},{48,32},{64,112},{80,64},{96,80},{112,96},{1... | collective-permute-start | bytes 196616 | tf_op jit(solution)/shard_map/ppermute | solution.py:395
  14.7 5.8 %collective-permute-start.4 = (f32[64,256]{1,0:T(8,128)S(1)}, f32[64,256]{1,0:T(8,128)S(1)}, u32[]{:S(2)}, u32[]{:S(2)}) collective-permute-start(f32[64,256]{1,0:T(8,128)S(1)} %get-tuple-element.49), channel_id=1, source_target_pairs={{0,32},{16,48},{32,0},{48,16},{64,96},{80,112},{96,64},{112,80},{1... | collective-permute-start | bytes 196616 | tf_op jit(solution)/shard_map/ppermute | solution.py:395
  20.4 5.9 %collective-permute-start.3 = (f32[64,256]{1,0:T(8,128)S(1)}, f32[64,256]{1,0:T(8,128)S(1)}, u32[]{:S(2)}, u32[]{:S(2)}) collective-permute-start(f32[64,256]{1,0:T(8,128)S(1)} %get-tuple-element.48), channel_id=1, source_target_pairs={{0,16},{16,32},{32,48},{48,0},{64,80},{80,96},{96,112},{112,64},{1... | collective-permute-start | bytes 196616 | tf_op jit(solution)/shard_map/ppermute | solution.py:395
  27.7 13.9 %collective-permute-start.7 = (f32[32,256]{1,0:T(8,128)S(1)}, f32[32,256]{1,0:T(8,128)S(1)}, u32[]{:S(2)}, u32[]{:S(2)}) collective-permute-start(f32[32,256]{1,0:T(8,128)S(1)} %bitcast_add_fusion), channel_id=1, source_target_pairs={{0,8},{1,9},{2,10},{3,11},{4,12},{5,13},{6,14},{7,15},{8,0},{9,1},... | collective-permute-start | bytes 98312 | tf_op jit(solution)/shard_map/ppermute | solution.py:392
  41.7 80.0 %all-to-all-start = ((f32[8,16,12544]{2,1,0:T(8,128)}), f32[8,16,12544]{2,1,0:T(8,128)}, u32[]{:S(2)}, u32[]{:S(2)}) async-start(f32[8,16,12544]{2,1,0:T(8,128)} %shard_map.55), calls=%async_computation | async-start | bytes 12845056 | tf_op jit(solution)/shard_map/all_to_all | solution.py:433
  48.6 4.9 %collective-permute-start.11 = (f32[2,784,256]{2,1,0:T(8,128)S(1)}, f32[2,784,256]{2,1,0:T(8,128)S(1)}, u32[]{:S(2)}, u32[]{:S(2)}) collective-permute-start(f32[2,784,256]{2,1,0:T(8,128)S(1)} %collective-permute-done.refs_9_), channel_id=1, source_target_pairs={{0,1},{1,0},{2,3},{3,2},{4,5},{5,4},{6,7},{7,6},{8,9},{9,8},{10,11... | collective-permute-start | bytes 4816904 | tf_op jit(solution)/shard_map/ppermute | solution.py:392
  48.6 7.9 %collective-permute-start.12 = (f32[2,784,256]{2,1,0:T(8,128)}, f32[2,784,256]{2,1,0:T(8,128)S(1)}, u32[]{:S(2)}, u32[]{:S(2)}) collective-permute-start(f32[2,784,256]{2,1,0:T(8,128)} %collective-permute-done.1.refs_5_), channel_id=1, source_target_pairs={{0,1},{1,0},{2,3},{3,2},{4,5},{5,4},{6,7},{7,6},{8,9},{9,8},{10,11... | collective-permute-start | bytes 4816904 | tf_op jit(solution)/shard_map/ppermute | solution.py:392
  49.1 7.5 %collective-permute-start.13 = (f32[2,784,256]{2,1,0:T(8,128)S(1)}, f32[2,784,256]{2,1,0:T(8,128)S(1)}, u32[]{:S(2)}, u32[]{:S(2)}) collective-permute-start(f32[2,784,256]{2,1,0:T(8,128)S(1)} %collective-permute-done.2.refs_3_), channel_id=1, source_target_pairs={{0,1},{1,0},{2,3},{3,2},{4,5},{5,4},{6,7},{7,6},{8,9},{9,8},{10,11... | collective-permute-start | bytes 4816904 | tf_op jit(solution)/shard_map/ppermute | solution.py:392
  49.2 41.5 %collective-permute-start.9 = (f32[2,784,256]{2,1,0:T(8,128)S(1)}, f32[2,784,256]{2,1,0:T(8,128)}, u32[]{:S(2)}, u32[]{:S(2)}) collective-permute-start(f32[2,784,256]{2,1,0:T(8,128)S(1)} %collective-permute-done.2.refs_3_), channel_id=1, source_target_pairs={{0,6},{1,7},{2,0},{3,1},{4,2},{5,3},{6,4},{7,5},{8,14},{9,15},{10,... | collective-permute-start | bytes 4816904 | tf_op jit(solution)/shard_map/ppermute | solution.py:392
  51.0 39.8 %collective-permute-start.10 = (f32[2,784,256]{2,1,0:T(8,128)S(1)}, f32[2,784,256]{2,1,0:T(8,128)}, u32[]{:S(2)}, u32[]{:S(2)}) collective-permute-start(f32[2,784,256]{2,1,0:T(8,128)S(1)} %collective-permute-done.refs_9_), channel_id=1, source_target_pairs={{0,2},{1,3},{2,4},{3,5},{4,6},{5,7},{6,0},{7,1},{8,10},{9,11},{10,... | collective-permute-start | bytes 4816904 | tf_op jit(solution)/shard_map/ppermute | solution.py:392
  58.0 29.7 %collective-permute-start.16 = (f32[32,256]{1,0:T(8,128)S(1)}, f32[32,256]{1,0:T(8,128)S(1)}, u32[]{:S(2)}, u32[]{:S(2)}) collective-permute-start(f32[32,256]{1,0:T(8,128)S(1)} %add.55), channel_id=1, source_target_pairs={{0,6},{1,7},{2,0},{3,1},{4,2},{5,3},{6,4},{7,5},{8,14},{9,15},{10,... | collective-permute-start | bytes 98312 | tf_op jit(solution)/shard_map/ppermute | solution.py:392
  59.7 29.4 %collective-permute-start.15 = (f32[32,256]{1,0:T(8,128)S(1)}, f32[32,256]{1,0:T(8,128)S(1)}, u32[]{:S(2)}, u32[]{:S(2)}) collective-permute-start(f32[32,256]{1,0:T(8,128)S(1)} %add.55), channel_id=1, source_target_pairs={{0,4},{1,5},{2,6},{3,7},{4,0},{5,1},{6,2},{7,3},{8,12},{9,13},{10,... | collective-permute-start | bytes 98312 | tf_op jit(solution)/shard_map/ppermute | solution.py:392
  59.8 30.9 %collective-permute-start.14 = (f32[32,256]{1,0:T(8,128)S(1)}, f32[32,256]{1,0:T(8,128)S(1)}, u32[]{:S(2)}, u32[]{:S(2)}) collective-permute-start(f32[32,256]{1,0:T(8,128)S(1)} %add.55), channel_id=1, source_target_pairs={{0,2},{1,3},{2,4},{3,5},{4,6},{5,7},{6,0},{7,1},{8,10},{9,11},{10,... | collective-permute-start | bytes 98312 | tf_op jit(solution)/shard_map/ppermute | solution.py:392
  90.8 30.8 %collective-permute-start.19 = (f32[2,784,256]{2,1,0:T(8,128)}, f32[2,784,256]{2,1,0:T(8,128)S(1)}, u32[]{:S(2)}, u32[]{:S(2)}) collective-permute-start(f32[2,784,256]{2,1,0:T(8,128)} %collective-permute-done.9.refs_5_), channel_id=1, source_target_pairs={{0,1},{1,0},{2,3},{3,2},{4,5},{5,4},{6,7},{7,6},{8,9},{9,8},{10,11... | collective-permute-start | bytes 4816904 | tf_op jit(solution)/shard_map/ppermute | solution.py:392
  90.9 30.8 %collective-permute-start.20 = (f32[2,784,256]{2,1,0:T(8,128)}, f32[2,784,256]{2,1,0:T(8,128)}, u32[]{:S(2)}, u32[]{:S(2)}) collective-permute-start(f32[2,784,256]{2,1,0:T(8,128)} %collective-permute-done.10.refs_7_), channel_id=1, source_target_pairs={{0,1},{1,0},{2,3},{3,2},{4,5},{5,4},{6,7},{7,6},{8,9},{9,8},{10,11... | collective-permute-start | bytes 4816904 | tf_op jit(solution)/shard_map/ppermute | solution.py:392
  91.4 40.4 %collective-permute-start.21 = (f32[2,784,256]{2,1,0:T(8,128)}, f32[2,784,256]{2,1,0:T(8,128)}, u32[]{:S(2)}, u32[]{:S(2)}) collective-permute-start(f32[2,784,256]{2,1,0:T(8,128)} %collective-permute-done.9.refs_5_), channel_id=1, source_target_pairs={{0,6},{1,7},{2,0},{3,1},{4,2},{5,3},{6,4},{7,5},{8,14},{9,15},{10,... | collective-permute-start | bytes 4816904 | tf_op jit(solution)/shard_map/ppermute | solution.py:392
  91.6 40.1 %collective-permute-start.22 = (f32[2,784,256]{2,1,0:T(8,128)S(1)}, f32[2,784,256]{2,1,0:T(8,128)}, u32[]{:S(2)}, u32[]{:S(2)}) collective-permute-start(f32[2,784,256]{2,1,0:T(8,128)S(1)} %collective-permute-done.2.refs_3_), channel_id=1, source_target_pairs={{0,2},{1,3},{2,4},{3,5},{4,6},{5,7},{6,0},{7,1},{8,10},{9,11},{10,... | collective-permute-start | bytes 4816904 | tf_op jit(solution)/shard_map/ppermute | solution.py:392
  96.3 25.3 %collective-permute-start.18 = (f32[64,256]{1,0:T(8,128)S(1)}, f32[64,256]{1,0:T(8,128)S(1)}, u32[]{:S(2)}, u32[]{:S(2)}) collective-permute-start(f32[64,256]{1,0:T(8,128)S(1)} %maximum_select_fusion), channel_id=1, source_target_pairs={{0,64},{16,80},{32,96},{48,112},{64,0},{80,16},{96,32},{112,48},{1... | collective-permute-start | bytes 196616 | tf_op jit(solution)/shard_map/ppermute | solution.py:395
  121.6 10.1 %collective-permute-start.23 = (f32[64,256]{1,0:T(8,128)S(1)}, f32[64,256]{1,0:T(8,128)S(1)}, u32[]{:S(2)}, u32[]{:S(2)}) collective-permute-start(f32[64,256]{1,0:T(8,128)S(1)} %add.59.refs_0_), channel_id=1, source_target_pairs={{0,16},{16,32},{32,48},{48,0},{64,80},{80,96},{96,112},{112,64},{1... | collective-permute-start | bytes 196616 | tf_op jit(solution)/shard_map/ppermute | solution.py:395
  123.2 8.6 %collective-permute-start.24 = (f32[64,256]{1,0:T(8,128)S(1)}, f32[64,256]{1,0:T(8,128)S(1)}, u32[]{:S(2)}, u32[]{:S(2)}) collective-permute-start(f32[64,256]{1,0:T(8,128)S(1)} %add.59.refs_0_), channel_id=1, source_target_pairs={{0,32},{16,48},{32,0},{48,16},{64,96},{80,112},{96,64},{112,80},{1... | collective-permute-start | bytes 196616 | tf_op jit(solution)/shard_map/ppermute | solution.py:395
  126.2 5.6 %collective-permute-start.25 = (f32[64,256]{1,0:T(8,128)S(1)}, f32[64,256]{1,0:T(8,128)S(1)}, u32[]{:S(2)}, u32[]{:S(2)}) collective-permute-start(f32[64,256]{1,0:T(8,128)S(1)} %add.59.refs_0_), channel_id=1, source_target_pairs={{0,48},{16,0},{32,16},{48,32},{64,112},{80,64},{96,80},{112,96},{1... | collective-permute-start | bytes 196616 | tf_op jit(solution)/shard_map/ppermute | solution.py:395
  131.9 6.0 %collective-permute-start.27 = (f32[2,784,256]{2,1,0:T(8,128)}, f32[2,784,256]{2,1,0:T(8,128)S(1)}, u32[]{:S(2)}, u32[]{:S(2)}) collective-permute-start(f32[2,784,256]{2,1,0:T(8,128)} %collective-permute-done.22.refs_9_), channel_id=1, source_target_pairs={{0,1},{1,0},{2,3},{3,2},{4,5},{5,4},{6,7},{7,6},{8,9},{9,8},{10,11... | collective-permute-start | bytes 4816904 | tf_op jit(solution)/shard_map/ppermute | solution.py:392
  146.3 7.0 %collective-permute-start.28 = (f32[32,512]{1,0:T(8,128)S(1)}, f32[32,512]{1,0:T(8,128)S(1)}, u32[]{:S(2)}, u32[]{:S(2)}) collective-permute-start(f32[32,512]{1,0:T(8,128)S(1)} %get-tuple-element.78), channel_id=1, source_target_pairs={{0,16},{16,32},{32,48},{48,0},{64,80},{80,96},{96,112},{112,64},{1... | collective-permute-start | bytes 196616 | tf_op jit(solution)/shard_map/ppermute | solution.py:395
  147.3 6.0 %collective-permute-start.29 = (f32[32,512]{1,0:T(8,128)S(1)}, f32[32,512]{1,0:T(8,128)S(1)}, u32[]{:S(2)}, u32[]{:S(2)}) collective-permute-start(f32[32,512]{1,0:T(8,128)S(1)} %get-tuple-element.79), channel_id=1, source_target_pairs={{0,32},{16,48},{32,0},{48,16},{64,96},{80,112},{96,64},{112,80},{1... | collective-permute-start | bytes 196616 | tf_op jit(solution)/shard_map/ppermute | solution.py:395
  149.0 4.9 %collective-permute-start.30 = (f32[32,512]{1,0:T(8,128)S(1)}, f32[32,512]{1,0:T(8,128)S(1)}, u32[]{:S(2)}, u32[]{:S(2)}) collective-permute-start(f32[32,512]{1,0:T(8,128)S(1)} %get-tuple-element.80), channel_id=1, source_target_pairs={{0,48},{16,0},{32,16},{48,32},{64,112},{80,64},{96,80},{112,96},{1... | collective-permute-start | bytes 196616 | tf_op jit(solution)/shard_map/ppermute | solution.py:395
  153.9 5.8 %collective-permute-start.31 = (f32[32,512]{1,0:T(8,128)S(1)}, f32[32,512]{1,0:T(8,128)S(1)}, u32[]{:S(2)}, u32[]{:S(2)}) collective-permute-start(f32[32,512]{1,0:T(8,128)S(1)} %shard_map.60.mine_ref), channel_id=1, source_target_pairs={{0,64},{16,80},{32,96},{48,112},{64,0},{80,16},{96,32},{112,48},{1... | collective-permute-start | bytes 196616 | tf_op jit(solution)/shard_map/ppermute | solution.py:395
  160.4 5.5 %collective-permute-start.32 = (f32[32,512]{1,0:T(8,128)S(1)}, f32[32,512]{1,0:T(8,128)S(1)}, u32[]{:S(2)}, u32[]{:S(2)}) collective-permute-start(f32[32,512]{1,0:T(8,128)S(1)} %shard_map.62.refs_2_), channel_id=1, source_target_pairs={{0,16},{16,32},{32,48},{48,0},{64,80},{80,96},{96,112},{112,64},{1... | collective-permute-start | bytes 196616 | tf_op jit(solution)/shard_map/ppermute | solution.py:395
  161.5 6.0 %collective-permute-start.33 = (f32[32,512]{1,0:T(8,128)S(1)}, f32[32,512]{1,0:T(8,128)S(1)}, u32[]{:S(2)}, u32[]{:S(2)}) collective-permute-start(f32[32,512]{1,0:T(8,128)S(1)} %shard_map.62.refs_2_), channel_id=1, source_target_pairs={{0,32},{16,48},{32,0},{48,16},{64,96},{80,112},{96,64},{112,80},{1... | collective-permute-start | bytes 196616 | tf_op jit(solution)/shard_map/ppermute | solution.py:395
  (14 other events, 193.0 us)
